TPU v7x, 512 devices: a whole 4x4x16 slice. The times are simulated.
512 devices in a mesh: freq: 32 (over z_lo, y), stn: 16 (over x, z_hi, core).
Axes of the slice: x: 4, y: 4, z: 16 (z_hi: 2, z_lo: 8; z = z_hi * 8 + z_lo), core: 2. Of those that a mesh axis runs over, the one named last changes fastest.
Arguments:
- voltages: bfloat16 [2, 1024, 524288], P(None, 'stn', 'freq'), may hold values from -6 to 6
Outputs:
- visibilities: float32 [32, 2, 1024, 1024], P('freq', None, 'stn')
All inputs are finite; a program needn't handle non-finite values.
Results may differ from a plain program's by a relative error of at most 0.0049.
Values may be sent and summed in bfloat16 or wider, within the bound.
No kernel may reach another device: no remote copies, remote signals or barrier semaphores. Data moves between devices by JAX's collectives and lax.ppermute only.
A program may use at most 128 MiB of HBM per device.

v0:
```python
import jax
import jax.numpy as jnp
from jax import lax
from jax.sharding import PartitionSpec as P

F = 4096
TAPS = 16
CH_DEV = 1


def make_taps(taps_count, points):
    j = jnp.arange(taps_count * points).astype(jnp.float32)
    total = float(taps_count * points)
    proto = jnp.sinc((j - total / 2.0 + 0.5) / points) * (
        0.5 - 0.5 * jnp.cos(2.0 * jnp.pi * (j + 0.5) / total)
    )
    proto = proto.reshape(taps_count, points)
    return proto / jnp.sqrt(jnp.sum(proto * proto, axis=0, keepdims=True))


def make_table(points, first, count):
    index = jnp.arange(points)
    chans = first + jnp.arange(count)
    turns = (index[:, None] * chans[None, :] % points).astype(jnp.float32)
    phase = 2.0 * jnp.pi * turns / points
    scale = points ** (-0.5)
    cosine = jnp.cos(phase) * scale
    sine = jnp.sin(phase) * scale
    upper = jnp.stack([cosine, -sine], axis=2).reshape(points, 2 * count)
    lower = jnp.stack([sine, cosine], axis=2).reshape(points, 2 * count)
    return jnp.concatenate([upper, lower], axis=0).astype(jnp.bfloat16)


def channelize(block, taps, table, spectra_count):
    parts, inputs_here, length = block.shape
    points = taps.shape[1]
    samples = block.astype(jnp.float32).reshape(parts, inputs_here, length // points, points)
    filtered = taps[0] * samples[:, :, 0:spectra_count, :]
    for k in range(1, taps.shape[0]):
        filtered = filtered + taps[k] * samples[:, :, k : k + spectra_count, :]
    rows = jnp.transpose(filtered, (2, 1, 0, 3)).reshape(spectra_count * inputs_here, 2 * points)
    spectra = jnp.dot(
        rows,
        table.astype(jnp.float32),
        precision=lax.Precision.HIGHEST,
        preferred_element_type=jnp.float32,
    ).astype(jnp.bfloat16)
    count = table.shape[1] // 2
    spectra = spectra.reshape(spectra_count, inputs_here, count, 2)
    return jnp.transpose(spectra, (1, 2, 3, 0))


def cross_products(left, right, spectra_count):
    full = jnp.einsum("crti,cstj->crsij", left, right, preferred_element_type=jnp.float32)
    real_part = full[:, 0, 0] + full[:, 1, 1]
    imag_part = full[:, 1, 0] - full[:, 0, 1]
    return jnp.stack([real_part, imag_part], axis=1) * (1.0 / spectra_count)


def body(voltages):
    freq_size = lax.axis_size("freq")
    stn_size = lax.axis_size("stn")
    keep = CH_DEV * freq_size
    offset = (F - keep) // 2
    blocks_here = voltages.shape[2] // F
    block_count = blocks_here * freq_size
    spectra_count = block_count - TAPS + 1
    in_stn = voltages.shape[1]
    in_freq = in_stn // freq_size
    taps = make_taps(TAPS, F)
    table = make_table(F, offset, keep)
    by_input = lax.all_to_all(voltages, "freq", split_axis=1, concat_axis=2, tiled=True)
    leading = channelize(by_input, taps, table, spectra_count)
    stations = lax.all_gather(leading, "stn", axis=0, tiled=True)
    turned = lax.all_to_all(stations, "freq", split_axis=1, concat_axis=0, tiled=True)
    turned = turned.reshape(freq_size, stn_size, in_freq, CH_DEV, 2, spectra_count)
    turned = jnp.transpose(turned, (3, 4, 5, 1, 0, 2)).reshape(
        CH_DEV, 2, spectra_count, stn_size * in_stn
    )
    first = lax.axis_index("stn") * in_stn
    mine = lax.dynamic_slice_in_dim(turned, first, in_stn, 3)
    return cross_products(mine, turned, spectra_count)


def solution(mesh):
    in_specs = (P(None, "stn", "freq"),)
    out_specs = P("freq", None, "stn", None)
    return jax.shard_map(body, mesh=mesh, in_specs=in_specs, out_specs=out_specs, check_vma=False)
```

profile of v0, /device:TPU:1, one launch (start us, length us, event | category | flops | bytes accessed | tf_op | source)
XLA Modules:
  0.0 1540.1 jit_solution(2758367945138778355)
XLA Ops:
  0.0 8.5 copy.45
  8.5 16.2 %all-to-all-start = ((bf16[2,64,16384]{2,0,1:T(2,128)(2,1)}), bf16[2,64,16384]{2,0,1:T(2,128)(2,1)}, u32[]{:S(2)}, u32[]{:S(2)}) async-start(bf16[2,64,16384]{2,0,1:T(2,128)(2,1)} %copy.45), calls=%async_computation | async-start | bytes 8388608 | tf_op jit(solution)/shard_map/all_to_all | solution.py:72
  24.7 1.5 multiply_reduce_fusion
  26.2 2.5 negate_convert_fusion
  28.7 0.1 pad_maximum_fusion
  28.8 0.5 copy.48
  29.4 0.2 reshape.287
  29.6 0.5 copy.49
  30.1 0.2 reshape.288
  30.3 1.2 broadcast_divide_fusion
  31.6 0.2 fusion.46
  31.8 178.9 %all-to-all-done = bf16[2,64,16384]{2,0,1:T(2,128)(2,1)} async-done(((bf16[2,64,16384]{2,0,1:T(2,128)(2,1)}), bf16[2,64,16384]{2,0,1:T(2,128)(2,1)}, u32[]{:S(2)}, u32[]{:S(2)}) %all-to-all-start) | async-done | bytes 4194336 | tf_op jit(solution)/shard_map/all_to_all | solution.py:72
  210.7 7.9 copy.65
  218.6 9.8 reshape.294
  228.4 52.2 %fusion.1 = f32[113,2,2,4096]{3,0,1,2:T(8,128)} fusion(f32[2,2,128,4096]{3,2,1,0:T(8,128)} %reshape.294, f32[4096]{0:T(1024)S(1)} %bitcast.80, f32[4096]{0:T(1024)S(1)} %bitcast.81, f32[4096]{0:T(1024)S(1)} %bitcast.82, f32[4096]{0:T(1024)S(1)} %bitcast.83, f32[4096]{0:T(1024)S(1)} %bitcast.84, f32[4096]{0:T(1024)S(1)} %bitcast.85, f32[4096]{0:T(1024)S(1)} %bitcast.86, ...), kind=kLoop, calls=%fused_computation.3 | loop fusion | flops 57393152 | bytes 126156800 | tf_op jit(solution)/shard_map/transpose | solution.py:41
  280.7 12.0 copy.47
  292.7 13.1 pad.8
  305.8 10.4 copy.63
  316.2 4.1 convolution_convert_fusion
  320.3 0.1 copy.50
  320.4 4.0 reshape.289
  324.5 981.5 %all_gather.3 = bf16[32,32,2,113]{2,1,0,3:T(8,128)(2,1)} all-gather(bf16[2,32,2,113]{2,1,0,3:T(8,128)(2,1)S(1)} %bitcast.75), channel_id=1, replica_groups=mesh['freq'=32,'stn'=16] {'stn'}, dimensions={0}, use_global_device_ids=true | all-gather | bytes 491776 | tf_op jit(solution)/shard_map/all_gather | solution.py:74
  1305.9 31.3 %copy.51 = bf16[32,32,2,113]{3,0,2,1:T(8,128)(2,1)} copy(bf16[32,32,2,113]{2,1,0,3:T(8,128)(2,1)} %all_gather.3) | data formatting | bytes 925696 | tf_op jit(solution)/shard_map/all_gather | solution.py:74
  1337.3 172.9 %all-to-all-start.1 = ((bf16[32,32,2,113]{3,0,2,1:T(8,128)(2,1)}), bf16[32,32,2,113]{3,0,2,1:T(8,128)(2,1)S(1)}, u32[]{:S(2)}, u32[]{:S(2)}) async-start(bf16[32,32,2,113]{3,0,2,1:T(8,128)(2,1)} %copy.51), calls=%async_computation.1 | async-start | bytes 1048576 | tf_op jit(solution)/shard_map/all_to_all | solution.py:75
  1510.2 27.6 %all-to-all-done.1 = bf16[32,32,2,113]{3,0,2,1:T(8,128)(2,1)S(1)} async-done(((bf16[32,32,2,113]{3,0,2,1:T(8,128)(2,1)}), bf16[32,32,2,113]{3,0,2,1:T(8,128)(2,1)S(1)}, u32[]{:S(2)}, u32[]{:S(2)}) %all-to-all-start.1) | async-done | bytes 462880 | tf_op jit(solution)/shard_map/all_to_all | solution.py:75
  1537.8 0.3 copy.52
  1538.1 0.5 copy.53
  1538.7 0.3 convolution_bitcast_fusion
  1539.1 0.8 maximum_multiply_fusion
  (4 shorter events, 0.1 us)
Async XLA Ops:
  8.5 202.2 %all-to-all-start = ((bf16[2,64,16384]{2,0,1:T(2,128)(2,1)}), bf16[2,64,16384]{2,0,1:T(2,128)(2,1)}, u32[]{:S(2)}, u32[]{:S(2)}) async-start(bf16[2,64,16384]{2,0,1:T(2,128)(2,1)} %copy.45), calls=%async_computation | async-start | bytes 8388608 | tf_op jit(solution)/shard_map/all_to_all | solution.py:72
  1337.3 200.5 %all-to-all-start.1 = ((bf16[32,32,2,113]{3,0,2,1:T(8,128)(2,1)}), bf16[32,32,2,113]{3,0,2,1:T(8,128)(2,1)S(1)}, u32[]{:S(2)}, u32[]{:S(2)}) async-start(bf16[32,32,2,113]{3,0,2,1:T(8,128)(2,1)} %copy.51), calls=%async_computation.1 | async-start | bytes 1048576 | tf_op jit(solution)/shard_map/all_to_all | solution.py:75
where the time goes:
time: 1560 us; the launch traced here: 1540 us
  blocking collectives  981 us (63%)
  waiting for transfers between devices  206 us (13%)
  starting transfers between devices  189 us (12%)
  local copies, waits for them, and re-layouts  99.8 us (6%)
  other arithmetic  58.5 us (4%)
    all_gather x1, blocking collectives, body(): stations = lax.all_gather(leading, 'stn', axis=0, tiled=True)  981 us
    all_to_all x1, waiting for transfers between devices, body(): lax.all_to_all(voltages, 'freq', split_axis=1, concat_axis=2, tiled=True)  179 us
    all_to_all x1, starting transfers between devices, body(): lax.all_to_all(stations, 'freq', split_axis=1, concat_axis=0, tiled=True)  173 us
    transpose x1, other arithmetic, channelize(): jnp.transpose(filtered, (2, 1, 0, 3))  52.2 us
    unnamed x3, local copies, waits for them, and re-layouts  32 us
    all_gather x1, local copies, waits for them, and re-layouts, body(): stations = lax.all_gather(leading, 'stn', axis=0, tiled=True)  31.3 us
  transfers between devices with their start and end apart: 2, of which 2 were waited for; matrix products, arithmetic and copies ran while one was open for 0% of the time, Pallas kernels for 0%

commit v1 on v0

v1 whole, which is shorter than its diff:
```python
import functools

import jax
import jax.numpy as jnp
import numpy as np
from jax import lax
from jax.experimental import pallas as pl
from jax.experimental.pallas import tpu as pltpu
from jax.sharding import PartitionSpec as P

F = 4096
TAPS = 16
NS = 113
KEEP = 32
OFFSET = 2032
BLOCKS = 4
PART = 24
CHUNK = 512
FINE = (7, 8)


def make_taps():
    j = np.arange(TAPS * F, dtype=np.float64)
    total = float(TAPS * F)
    proto = np.sinc((j - total / 2.0 + 0.5) / F) * (
        0.5 - 0.5 * np.cos(2.0 * np.pi * (j + 0.5) / total)
    )
    proto = proto.reshape(TAPS, F)
    return (proto / np.sqrt(np.sum(proto * proto, axis=0, keepdims=True))).astype(np.float32)


def make_table():
    turns = (OFFSET + np.arange(KEEP))[:, None] * np.arange(F)[None, :] % F
    phase = 2.0 * np.pi * turns / F
    both = np.concatenate([np.cos(phase), np.sin(phase)], axis=0) * F**-0.5
    return both.astype(np.float32).astype(jnp.bfloat16)


def channelize_kernel(x0, x1, x2, x3, taps_ref, table_ref, out_ref, acc, parts):
    step = pl.program_id(0)
    table = table_ref[...].astype(jnp.float32)
    coarse, fine = [], []
    for k in range(TAPS):
        weight = table * taps_ref[k : k + 1, :]
        high = weight.astype(jnp.bfloat16)
        coarse.append(high)
        if k in FINE:
            fine.append((weight - high.astype(jnp.float32)).astype(jnp.bfloat16))
    weights = jnp.concatenate(coarse + fine, axis=0)
    samples = jnp.concatenate([x0[...], x1[...], x2[...], x3[...]], axis=0)
    product = lax.dot_general(
        weights, samples, (((1,), (1,)), ((), ())), preferred_element_type=jnp.float32
    )

    @pl.when(step == 0)
    def _():
        acc[...] = product

    @pl.when(step > 0)
    def _():
        acc[...] += product

    @pl.when(step == pl.num_programs(0) - 1)
    def _():
        lane = lax.broadcasted_iota(jnp.int32, (KEEP, 128), 1)
        sign = jnp.where(lane < 64, 1.0, -1.0).astype(jnp.float32)
        for m in range(BLOCKS + TAPS - 1):
            cosine = jnp.zeros((KEEP, 128), jnp.float32)
            sine = jnp.zeros((KEEP, 128), jnp.float32)
            for b in range(BLOCKS):
                k = b + TAPS - 1 - m
                if not 0 <= k < TAPS:
                    continue
                rows = [2 * KEEP * k]
                if k in FINE:
                    rows.append(2 * KEEP * (TAPS + FINE.index(k)))
                for row in rows:
                    cosine += acc[row : row + KEEP, 128 * b : 128 * (b + 1)]
                    sine += acc[row + KEEP : row + 2 * KEEP, 128 * b : 128 * (b + 1)]
            parts[m] = cosine + sign * pltpu.roll(sine, 64, 1)
        for m in range(BLOCKS + TAPS - 1, PART):
            parts[m] = jnp.zeros((KEEP, 128), jnp.float32)
        out_ref[...] = jnp.swapaxes(parts[...], 0, 1).astype(jnp.bfloat16)


def channelize(voltages, taps, table):
    samples = voltages.reshape(128, BLOCKS * F)
    steps = F // CHUNK
    block = lambda b: pl.BlockSpec((128, CHUNK), lambda j, b=b: (0, b * steps + j))
    return pl.pallas_call(
        channelize_kernel,
        grid=(steps,),
        in_specs=[block(b) for b in range(BLOCKS)]
        + [
            pl.BlockSpec((TAPS, CHUNK), lambda j: (0, j)),
            pl.BlockSpec((2 * KEEP, CHUNK), lambda j: (0, j)),
        ],
        out_specs=pl.BlockSpec((KEEP, PART, 128), lambda j: (0, 0, 0)),
        out_shape=jax.ShapeDtypeStruct((KEEP, PART, 128), jnp.bfloat16),
        scratch_shapes=[
            pltpu.VMEM((2 * KEEP * (TAPS + len(FINE)), BLOCKS * 128), jnp.float32),
            pltpu.VMEM((PART, KEEP, 128), jnp.float32),
        ],
        compiler_params=pltpu.CompilerParams(
            dimension_semantics=("arbitrary",), vmem_limit_bytes=40 * 1024 * 1024
        ),
        name="channelize",
    )(samples, samples, samples, samples, taps, table)


def overlap_kernel(recv_ref, out_ref, wide):
    wide[...] = recv_ref[...].astype(jnp.float32).reshape(KEEP * PART, 128)
    block = lax.broadcasted_iota(jnp.int32, (KEEP, 128), 0)
    for r in range(BLOCKS):
        total = jnp.zeros((KEEP, 128), jnp.float32)
        for a in range((TAPS - 1 + BLOCKS - 1) // BLOCKS + 1):
            m = BLOCKS * a + r
            if m >= BLOCKS + TAPS - 1:
                continue
            share = wide[pl.ds(m, KEEP, stride=PART), :]
            if a:
                share = jnp.where(block >= a, pltpu.roll(share, a, 0), 0.0)
            total += share
        total = jnp.where(BLOCKS * block + r >= TAPS - 1, total, 0.0)
        out_ref[KEEP * r : KEEP * (r + 1), :] = total.astype(jnp.bfloat16)


def overlap(recv):
    return pl.pallas_call(
        overlap_kernel,
        out_shape=jax.ShapeDtypeStruct((BLOCKS * KEEP, 128), jnp.bfloat16),
        scratch_shapes=[pltpu.VMEM((KEEP * PART, 128), jnp.float32)],
        name="overlap",
    )(recv)


def products_kernel(mine_ref, all_ref, out_ref):
    mine = mine_ref[...].astype(jnp.float32)
    lane = lax.broadcasted_iota(jnp.int32, mine.shape, 1)
    turned = pltpu.roll(mine, 64, 1) * jnp.where(lane < 64, 1.0, -1.0)
    left = jnp.concatenate([mine, turned], axis=0).astype(jnp.bfloat16)
    first = lane < 64
    for pair in range(all_ref.shape[0] // 2):
        one = all_ref[2 * pair].astype(jnp.float32)
        two = all_ref[2 * pair + 1].astype(jnp.float32)
        real = jnp.where(first, one, pltpu.roll(two, 64, 1))
        imag = jnp.where(first, pltpu.roll(one, 64, 1), two)
        right = jnp.concatenate([real, imag], axis=0).astype(jnp.bfloat16)
        full = lax.dot_general(
            left, right, (((0,), (0,)), ((), ())), preferred_element_type=jnp.float32
        ) * (1.0 / NS)
        out_ref[0, 0, :, 128 * pair : 128 * (pair + 1)] = full[:64]
        out_ref[0, 1, :, 128 * pair : 128 * (pair + 1)] = full[64:]


def products(mine, everyone):
    return pl.pallas_call(
        products_kernel,
        out_shape=jax.ShapeDtypeStruct((1, 2, 64, 64 * everyone.shape[0]), jnp.float32),
        name="products",
    )(mine, everyone)


def body(voltages):
    taps = jnp.asarray(make_taps())
    table = jnp.asarray(make_table())
    sent = channelize(voltages, taps, table)
    recv = lax.all_to_all(sent, "freq", split_axis=0, concat_axis=0, tiled=True)
    mine = overlap(recv)
    everyone = lax.all_gather(mine, "stn", axis=0)
    return products(mine, everyone)


def solution(mesh):
    return jax.shard_map(
        body,
        mesh=mesh,
        in_specs=(P(None, "stn", "freq"),),
        out_specs=P("freq", None, "stn", None),
        check_vma=False,
    )
```

time: 1560 us -> 100 us (0.06)
  the two profiles are of different devices: /device:TPU:1 before, /device:TPU:33 now
where the time goes in v1:
time: 100 us; the launch traced here: 99.9 us
  blocking collectives  82.8 us (83%)
  Pallas kernels  13 us (13%)
  local copies, waits for them, and re-layouts  4.18 us (4%)
    all_gather x1, blocking collectives, body(): everyone = lax.all_gather(mine, 'stn', axis=0)  56.4 us
    all_to_all x1, blocking collectives, body(): recv = lax.all_to_all(sent, 'freq', split_axis=0, concat_axis=0, tiled=True)  26.4 us
    pallas_call x1, Pallas kernels, channelize(): pl.pallas_call(channelize_kernel, grid=(steps,), in_specs=[block(b) for b...  9.05 us
    unnamed x6, local copies, waits for them, and re-layouts  4.18 us
    pallas_call x1, Pallas kernels, products(): pl.pallas_call(products_kernel, out_shape=jax.ShapeDtypeStruct((1, 2, 64,...  2.29 us

profile of v1, /device:TPU:33, one launch (start us, length us, event | category | flops | bytes accessed | tf_op | source)
XLA Modules:
  0.0 99.9 jit_solution(16093944209558775279)
XLA Ops:
  0.0 0.0 copy-start
  0.0 2.2 %copy-done = bf16[2,64,16384]{2,1,0:T(8,128)(2,1)S(1)} copy-done((bf16[2,64,16384]{2,1,0:T(8,128)(2,1)S(1)}, bf16[2,64,16384]{2,1,0:T(8,128)(2,1)}, u32[]{:S(2)}) %copy-start) | copy-done | bytes 4194328
  2.2 0.0 copy-start.1
  2.2 1.0 %copy-done.1 = bf16[64,4096]{1,0:T(8,128)(2,1)S(1)} copy-done((bf16[64,4096]{1,0:T(8,128)(2,1)S(1)}, bf16[64,4096]{1,0:T(8,128)(2,1)}, u32[]{:S(2)}) %copy-start.1) | copy-done | bytes 524312
  3.2 0.0 copy-start.2
  3.2 0.9 copy-done.2
  4.2 9.0 %channelize.1 = bf16[32,24,128]{2,1,0:T(8,128)(2,1)S(1)} custom-call(bf16[128,16384]{1,0:T(8,128)(2,1)S(1)} %bitcast.2, bf16[128,16384]{1,0:T(8,128)(2,1)S(1)} %bitcast.3, bf16[128,16384]{1,0:T(8,128)(2,1)S(1)} %bitcast.4, bf16[128,16384]{1,0:T(8,128)(2,1)S(1)} %bitcast.5, f32[16,4096]{1,0:T(8,128)S(1)} %copy-done.2, bf16[64,4096]{1,0:T(8,128)(2,1)S(1)} %copy-done.1), custom_call_target="tpu_custom_call" | custom-call | tf_op jit(solution)/shard_map/channelize/pallas_call | solution.py:90
  13.2 26.4 %all_to_all.5.recv_ref = bf16[32,24,128]{2,1,0:T(8,128)(2,1)} all-to-all(bf16[32,24,128]{2,1,0:T(8,128)(2,1)S(1)} %channelize.1), channel_id=1, replica_groups=mesh['freq'=32,'stn'=16] {'freq'}, dimensions={0} | all-to-all | bytes 393216 | tf_op jit(solution)/shard_map/all_to_all | solution.py:168
  39.6 1.6 %overlap.1.mine_ref = bf16[128,128]{1,0:T(8,128)(2,1)} custom-call(bf16[32,24,128]{2,1,0:T(8,128)(2,1)} %all_to_all.5.recv_ref), custom_call_target="tpu_custom_call" | custom-call | tf_op jit(solution)/shard_map/overlap/pallas_call | solution.py:129
  41.2 56.4 %all-gather = bf16[2048,128]{1,0:T(8,128)(2,1)} all-gather(bf16[128,128]{1,0:T(8,128)(2,1)} %overlap.1.mine_ref), channel_id=2, replica_groups=mesh['freq'=32,'stn'=16] {'stn'}, dimensions={0}, use_global_device_ids=true | all-gather | bytes 557056 | tf_op jit(solution)/shard_map/all_gather | solution.py:170
  97.6 2.3 %products.1 = f32[1,2,64,1024]{3,2,1,0:T(8,128)} custom-call(bf16[128,128]{1,0:T(8,128)(2,1)} %overlap.1.mine_ref, bf16[16,128,128]{2,1,0:T(8,128)(2,1)} %bitcast.6), custom_call_target="tpu_custom_call" | custom-call | tf_op jit(solution)/shard_map/products/pallas_call | solution.py:157
Async XLA Ops:
  0.0 2.2 %copy-start = (bf16[2,64,16384]{2,1,0:T(8,128)(2,1)S(1)}, bf16[2,64,16384]{2,1,0:T(8,128)(2,1)}, u32[]{:S(2)}) copy-start(bf16[2,64,16384]{2,1,0:T(8,128)(2,1)} %param.3) | copy-start | bytes 12582916
  2.2 1.0 %copy-start.1 = (bf16[64,4096]{1,0:T(8,128)(2,1)S(1)}, bf16[64,4096]{1,0:T(8,128)(2,1)}, u32[]{:S(2)}) copy-start(bf16[64,4096]{1,0:T(8,128)(2,1)} %constant.5.clone.table_ref) | copy-start | bytes 1572868
  3.2 0.9 copy-start.2

commit v2 on v1

v2 whole, which is shorter than its diff:
```python
import jax
import jax.numpy as jnp
import numpy as np
from jax import lax
from jax.experimental import pallas as pl
from jax.experimental.pallas import tpu as pltpu
from jax.sharding import Mesh
from jax.sharding import PartitionSpec as P

F = 4096
TAPS = 16
NS = 113
KEEP = 32
HALF = KEEP // 2
MIDDLE = F // 2
BLOCKS = 4
GROUPS = 5
CHUNK = 1024
STEPS = F // CHUNK
FINE = (7, 8)
EDGE = KEEP * TAPS
FINES = EDGE + KEEP
FINE_EDGE = FINES + KEEP * len(FINE)
ROWS = FINE_EDGE + KEEP


def make_taps():
    j = np.arange(TAPS * F, dtype=np.float64)
    total = float(TAPS * F)
    proto = np.sinc((j - total / 2.0 + 0.5) / F) * (
        0.5 - 0.5 * np.cos(2.0 * np.pi * (j + 0.5) / total)
    )
    proto = proto.reshape(TAPS, F)
    taps = proto / np.sqrt(np.sum(proto * proto, axis=0, keepdims=True))
    return taps[::-1].astype(np.float32)


def make_table():
    turns = (MIDDLE + np.arange(HALF + 1))[:, None] * np.arange(F)[None, :] % F
    phase = 2.0 * np.pi * turns / F
    cosine, sine = np.cos(phase) * F**-0.5, np.sin(phase) * F**-0.5
    rows = [cosine[:HALF], sine[:HALF], cosine[HALF:], sine[HALF:], np.zeros((6, F))]
    table = np.concatenate(rows, axis=0).astype(np.float32)
    return table.astype(jnp.bfloat16).astype(np.float32)


def split(weight):
    high = weight.astype(jnp.bfloat16)
    return high, (weight - high.astype(jnp.float32)).astype(jnp.bfloat16)


def channelize_kernel(x_hbm, taps_hbm, table_hbm, out_ref, x, taps, table, acc, parts, sems):
    first = [
        pltpu.make_async_copy(taps_hbm, taps, sems.at[0]),
        pltpu.make_async_copy(table_hbm, table, sems.at[1]),
    ]
    for copy in first:
        copy.start()
    copies = []
    for j in range(STEPS):
        for b in range(BLOCKS):
            at = pl.ds(b * F + j * CHUNK, CHUNK)
            copy = pltpu.make_async_copy(
                x_hbm.at[:, at], x.at[:, at], sems.at[2 + j * BLOCKS + b]
            )
            copy.start()
            copies.append(copy)
    for copy in first:
        copy.wait()

    for j in range(STEPS):
        here = slice(j * CHUNK, (j + 1) * CHUNK)
        tap = taps[:, here]
        wide = table[:, here]
        main, fine = [], []
        for i in range(TAPS):
            high, low = split(wide[:KEEP] * tap[i : i + 1])
            main.append(high)
            if i in FINE:
                fine.append(low)
        edge = jnp.concatenate([tap * wide[KEEP : KEEP + 1], tap * wide[KEEP + 1 : KEEP + 2]], axis=0)
        high, low = split(edge)
        weights = jnp.concatenate(main + [high] + fine + [low], axis=0)
        for copy in copies[j * BLOCKS : (j + 1) * BLOCKS]:
            copy.wait()
        samples = jnp.concatenate(
            [x[:, b * F + j * CHUNK : b * F + (j + 1) * CHUNK] for b in range(BLOCKS)], axis=0
        )
        product = lax.dot_general(
            weights, samples, (((1,), (1,)), ((), ())), preferred_element_type=jnp.float32
        )
        if j == 0:
            acc[...] = product
        else:
            acc[...] += product

    lane = lax.broadcasted_iota(jnp.int32, (1, 128), 1)
    sign = jnp.where(lane < 64, 1.0, -1.0).astype(jnp.float32)
    for m in range(GROUPS * BLOCKS):
        cosine = jnp.zeros((HALF, 128), jnp.float32)
        sine = jnp.zeros((HALF, 128), jnp.float32)
        for b in range(BLOCKS):
            i = m - b
            if not 0 <= i < TAPS:
                continue
            rows = [KEEP * i]
            if i in FINE:
                rows.append(FINES + KEEP * FINE.index(i))
            for row in rows:
                cosine += acc[row : row + HALF, 128 * b : 128 * (b + 1)]
                sine += acc[row + HALF : row + KEEP, 128 * b : 128 * (b + 1)]
        turned = sign * pltpu.roll(sine, 64, 1)
        parts[KEEP * m : KEEP * m + HALF, :] = cosine + turned
        parts[KEEP * m + HALF : KEEP * (m + 1), :] = cosine - turned

    def put(channel, group, rows):
        rows = rows.astype(jnp.bfloat16)
        out_ref[channel, group] = rows
        out_ref[KEEP + channel, group] = rows

    for p in range(HALF):
        for a in range(GROUPS):
            above = parts[pl.ds(KEEP * BLOCKS * a + p, BLOCKS, stride=KEEP), :]
            put(HALF + p, a, above)
            if p:
                below = parts[pl.ds(KEEP * BLOCKS * a + HALF + p, BLOCKS, stride=KEEP), :]
                put(HALF - p, a, below)
    edge = acc[EDGE:FINES, :] + acc[FINE_EDGE:ROWS, :]
    total = jnp.zeros((GROUPS * BLOCKS, 128), jnp.float32)
    for b in range(BLOCKS):
        cosine = edge[:TAPS, 128 * b : 128 * (b + 1)]
        sine = edge[TAPS:, 128 * b : 128 * (b + 1)]
        share = cosine - sign * pltpu.roll(sine, 64, 1)
        pieces = [share]
        if b:
            pieces.insert(0, jnp.zeros((b, 128), jnp.float32))
        if b < BLOCKS:
            pieces.append(jnp.zeros((BLOCKS - b, 128), jnp.float32))
        total += jnp.concatenate(pieces, axis=0)
    for a in range(GROUPS):
        put(0, a, total[BLOCKS * a : BLOCKS * (a + 1)])


def channelize(voltages, taps, table):
    samples = voltages.reshape(128, BLOCKS * F)
    samples, taps, table = (
        pltpu.with_memory_space_constraint(array, pltpu.HBM) for array in (samples, taps, table)
    )
    anywhere = pl.BlockSpec(memory_space=pltpu.HBM)
    return pl.pallas_call(
        channelize_kernel,
        in_specs=[anywhere] * 3,
        out_shape=jax.ShapeDtypeStruct((2 * KEEP, GROUPS, BLOCKS, 128), jnp.bfloat16),
        scratch_shapes=[
            pltpu.VMEM((128, BLOCKS * F), jnp.bfloat16),
            pltpu.VMEM((TAPS, F), jnp.float32),
            pltpu.VMEM((40, F), jnp.float32),
            pltpu.VMEM((ROWS, BLOCKS * 128), jnp.float32),
            pltpu.VMEM((GROUPS * BLOCKS * KEEP, 128), jnp.float32),
            pltpu.SemaphoreType.DMA((2 + STEPS * BLOCKS,)),
        ],
        compiler_params=pltpu.CompilerParams(vmem_limit_bytes=40 * 1024 * 1024),
        name="channelize",
    )(samples, taps, table)


def overlap_kernel(recv_ref, out_ref, wide):
    row = lax.broadcasted_iota(jnp.int32, (BLOCKS, 128), 0)
    for z in range(2):
        for d in range(KEEP):
            total = jnp.zeros((BLOCKS, 128), jnp.float32)
            if BLOCKS * (d + 1) >= TAPS:
                for a in range(min(d + 1, GROUPS)):
                    total += recv_ref[KEEP * z + d - a, a].astype(jnp.float32)
                if BLOCKS * d < TAPS - 1:
                    total = jnp.where(BLOCKS * d + row >= TAPS - 1, total, 0.0)
            at = KEEP * BLOCKS * z + BLOCKS * d
            wide[at : at + BLOCKS, :] = total
    done = wide[...].astype(jnp.bfloat16).reshape(2, BLOCKS * KEEP, 128)
    for x in range(out_ref.shape[0]):
        out_ref[x] = done


def overlap(recv, copies):
    return pl.pallas_call(
        overlap_kernel,
        out_shape=jax.ShapeDtypeStruct((copies, 2, BLOCKS * KEEP, 128), jnp.bfloat16),
        scratch_shapes=[pltpu.VMEM((2 * BLOCKS * KEEP, 128), jnp.float32)],
        name="overlap",
    )(recv)


def products_kernel(me_ref, all_ref, out_ref):
    mine = all_ref[me_ref[0], me_ref[1]].astype(jnp.float32)
    lane = lax.broadcasted_iota(jnp.int32, mine.shape, 1)
    turned = pltpu.roll(mine, 64, 1) * jnp.where(lane < 64, 1.0, -1.0)
    left = jnp.concatenate([mine, turned], axis=0).astype(jnp.bfloat16)
    first = lane < 64
    for pair in range(all_ref.shape[1]):
        one = all_ref[0, pair].astype(jnp.float32)
        two = all_ref[1, pair].astype(jnp.float32)
        real = jnp.where(first, one, pltpu.roll(two, 64, 1))
        imag = jnp.where(first, pltpu.roll(one, 64, 1), two)
        right = jnp.concatenate([real, imag], axis=0).astype(jnp.bfloat16)
        full = lax.dot_general(
            left, right, (((0,), (0,)), ((), ())), preferred_element_type=jnp.float32
        ) * (1.0 / NS)
        out_ref[0, 0, :, 128 * pair : 128 * (pair + 1)] = full[:64]
        out_ref[0, 1, :, 128 * pair : 128 * (pair + 1)] = full[64:]


def products(me, everyone):
    pairs = everyone.shape[1]
    return pl.pallas_call(
        products_kernel,
        in_specs=[
            pl.BlockSpec(memory_space=pltpu.SMEM),
            pl.BlockSpec(memory_space=pltpu.VMEM),
        ],
        out_shape=jax.ShapeDtypeStruct((1, 2, 64, 128 * pairs), jnp.float32),
        name="products",
    )(me, everyone)


def body(voltages):
    taps = jnp.asarray(make_taps())
    table = jnp.asarray(make_table())
    sent = channelize(voltages, taps, table)
    recv = lax.all_to_all(sent, ("zh", "zl", "y"), split_axis=0, concat_axis=0, tiled=True)
    mine = overlap(recv, 4)
    row = lax.all_to_all(mine, "x", split_axis=0, concat_axis=0, tiled=True)
    row = row.reshape(8, BLOCKS * KEEP, 128)
    everyone = lax.all_gather(row, "c", axis=0)
    me = jnp.stack([lax.axis_index("c"), 2 * lax.axis_index("x") + lax.axis_index("zh")])
    return products(me.astype(jnp.int32), everyone)


def solution(mesh):
    fine = Mesh(mesh.devices.reshape(8, 4, 4, 2, 2), ("zl", "y", "x", "zh", "c"))
    return jax.shard_map(
        body,
        mesh=fine,
        in_specs=(P(None, ("x", "zh", "c"), ("zl", "y")),),
        out_specs=P(("zl", "y"), None, ("x", "zh", "c"), None),
        check_vma=False,
    )
```

time: 100 us -> 68.1 us (0.68)
  the two profiles are of different devices: /device:TPU:33 before, /device:TPU:1 now
where the time goes in v2:
time: 68.1 us; the launch traced here: 67.8 us
  blocking collectives  48.5 us (71%)
  Pallas kernels  9.62 us (14%)
  waiting for transfers between devices  4.88 us (7%)
  starting transfers between devices  4.17 us (6%)
    all_to_all x1, blocking collectives, body(): lax.all_to_all(sent, ('zh', 'zl', 'y'), split_axis=0, concat_axis=0, tile...  41.3 us
    all_gather x1, blocking collectives, body(): everyone = lax.all_gather(row, 'c', axis=0)  7.24 us
    pallas_call x1, Pallas kernels, channelize(): pl.pallas_call(channelize_kernel, in_specs=[anywhere] * 3, out_shape=jax....  5.56 us
    all_to_all x1, waiting for transfers between devices, body(): row = lax.all_to_all(mine, 'x', split_axis=0, concat_axis=0, tiled=True)  4.88 us
    all_to_all x1, starting transfers between devices, body(): row = lax.all_to_all(mine, 'x', split_axis=0, concat_axis=0, tiled=True)  4.17 us
    pallas_call x1, Pallas kernels, products(): pl.pallas_call(products_kernel, in_specs=[pl.BlockSpec(memory_space=pltpu...  2.29 us
    pallas_call x1, Pallas kernels, overlap(): pl.pallas_call(overlap_kernel, out_shape=jax.ShapeDtypeStruct((copies, 2,...  1.77 us
  transfers between devices with their start and end apart: 1, of which 1 were waited for; matrix products, arithmetic and copies ran while one was open for 1% of the time, Pallas kernels for 0%

profile of v2, /device:TPU:1, one launch (start us, length us, event | category | flops | bytes accessed | tf_op | source)
XLA Modules:
  0.0 67.8 jit_solution(13783563832561597513)
XLA Ops:
  0.0 5.6 %channelize.1 = bf16[64,5,4,128]{3,2,1,0:T(4,128)(2,1)S(1)} custom-call(bf16[128,16384]{1,0:T(8,128)(2,1)} %bitcast.4, f32[16,4096]{1,0:T(8,128)} %constant.17.clone.taps_hbm, f32[40,4096]{1,0:T(8,128)} %constant.18.clone.table_hbm), custom_call_target="tpu_custom_call" | custom-call | tf_op jit(solution)/shard_map/channelize/pallas_call | solution.py:150
  5.6 41.3 %all_to_all.10.recv_ref = bf16[64,5,4,128]{3,2,1,0:T(4,128)(2,1)} all-to-all(bf16[64,5,4,128]{3,2,1,0:T(4,128)(2,1)S(1)} %channelize.1), channel_id=1, replica_groups=mesh['zl'=8,'y'=4,'x'=4,'zh'=2,'c'=2] {'zh','zl','y'}, dimensions={0} | all-to-all | bytes 655360 | tf_op jit(solution)/shard_map/all_to_all | solution.py:229
  46.8 1.8 %overlap.1 = bf16[4,2,128,128]{3,2,1,0:T(8,128)(2,1)} custom-call(bf16[64,5,4,128]{3,2,1,0:T(4,128)(2,1)} %all_to_all.10.recv_ref), custom_call_target="tpu_custom_call" | custom-call | tf_op jit(solution)/shard_map/overlap/pallas_call | solution.py:185
  48.6 4.2 %all-to-all-start.1 = ((bf16[4,2,128,128]{3,2,1,0:T(8,128)(2,1)}), bf16[4,2,128,128]{3,2,1,0:T(8,128)(2,1)S(1)}, u32[]{:S(2)}, u32[]{:S(2)}) async-start(bf16[4,2,128,128]{3,2,1,0:T(8,128)(2,1)} %overlap.1), calls=%async_computation.1 | async-start | bytes 524288 | tf_op jit(solution)/shard_map/all_to_all | solution.py:231
  52.8 0.7 pad_add_fusion.me_ref
  53.4 4.9 %all-to-all-done.1 = bf16[4,2,128,128]{3,2,1,0:T(8,128)(2,1)S(1)} async-done(((bf16[4,2,128,128]{3,2,1,0:T(8,128)(2,1)}), bf16[4,2,128,128]{3,2,1,0:T(8,128)(2,1)S(1)}, u32[]{:S(2)}, u32[]{:S(2)}) %all-to-all-start.1) | async-done | bytes 262176 | tf_op jit(solution)/shard_map/all_to_all | solution.py:231
  58.3 7.2 %all_gather.3.all_ref = bf16[2,8,128,128]{3,2,1,0:T(8,128)(2,1)} all-gather(bf16[1,8,128,128]{3,2,1,0:T(8,128)(2,1)S(1)} %bitcast.5), channel_id=1, replica_groups=mesh['zl'=8,'y'=4,'x'=4,'zh'=2,'c'=2] {'c'}, dimensions={0}, use_global_device_ids=true | all-gather | bytes 786432 | tf_op jit(solution)/shard_map/all_gather | solution.py:233
  65.5 2.3 %products.1 = f32[1,2,64,1024]{3,2,1,0:T(8,128)} custom-call(s32[2]{0:T(128)} %pad_add_fusion.me_ref, bf16[2,8,128,128]{3,2,1,0:T(8,128)(2,1)} %all_gather.3.all_ref), custom_call_target="tpu_custom_call" | custom-call | tf_op jit(solution)/shard_map/products/pallas_call | solution.py:214
Async XLA Ops:
  48.6 9.7 %all-to-all-start.1 = ((bf16[4,2,128,128]{3,2,1,0:T(8,128)(2,1)}), bf16[4,2,128,128]{3,2,1,0:T(8,128)(2,1)S(1)}, u32[]{:S(2)}, u32[]{:S(2)}) async-start(bf16[4,2,128,128]{3,2,1,0:T(8,128)(2,1)} %overlap.1), calls=%async_computation.1 | async-start | bytes 524288 | tf_op jit(solution)/shard_map/all_to_all | solution.py:231

commit v3 on v2

--- a/solution.py
+++ b/solution.py
@@ -15,8 +15,11 @@
 MIDDLE = F // 2
 BLOCKS = 4
 GROUPS = 5
-CHUNK = 1024
-STEPS = F // CHUNK
+ROW = 4
+LINE = KEEP // ROW
+SPAN = 32
+CUTS = (0, 512, 1536, 2816, 4096)
+STEPS = len(CUTS) - 1
 FINE = (7, 8)
 EDGE = KEEP * TAPS
 FINES = EDGE + KEEP
@@ -50,26 +53,25 @@
 
 
 def channelize_kernel(x_hbm, taps_hbm, table_hbm, out_ref, x, taps, table, acc, parts, sems):
-    first = [
-        pltpu.make_async_copy(taps_hbm, taps, sems.at[0]),
-        pltpu.make_async_copy(table_hbm, table, sems.at[1]),
-    ]
-    for copy in first:
-        copy.start()
     copies = []
     for j in range(STEPS):
+        size = CUTS[j + 1] - CUTS[j]
+        here = pl.ds(CUTS[j], size)
+        own = [
+            pltpu.make_async_copy(taps_hbm.at[:, here], taps.at[:, here], sems.at[j, 0]),
+            pltpu.make_async_copy(table_hbm.at[:, here], table.at[:, here], sems.at[j, 1]),
+        ]
         for b in range(BLOCKS):
-            at = pl.ds(b * F + j * CHUNK, CHUNK)
-            copy = pltpu.make_async_copy(
-                x_hbm.at[:, at], x.at[:, at], sems.at[2 + j * BLOCKS + b]
-            )
+            at = pl.ds(b * F + CUTS[j], size)
+            own.append(pltpu.make_async_copy(x_hbm.at[:, at], x.at[:, at], sems.at[j, 2 + b]))
+        for copy in own:
             copy.start()
-            copies.append(copy)
-    for copy in first:
-        copy.wait()
+        copies.append(own)
 
     for j in range(STEPS):
-        here = slice(j * CHUNK, (j + 1) * CHUNK)
+        here = slice(CUTS[j], CUTS[j + 1])
+        for copy in copies[j][:2]:
+            copy.wait()
         tap = taps[:, here]
         wide = table[:, here]
         main, fine = [], []
@@ -81,10 +83,10 @@
         edge = jnp.concatenate([tap * wide[KEEP : KEEP + 1], tap * wide[KEEP + 1 : KEEP + 2]], axis=0)
         high, low = split(edge)
         weights = jnp.concatenate(main + [high] + fine + [low], axis=0)
-        for copy in copies[j * BLOCKS : (j + 1) * BLOCKS]:
+        for copy in copies[j][2:]:
             copy.wait()
         samples = jnp.concatenate(
-            [x[:, b * F + j * CHUNK : b * F + (j + 1) * CHUNK] for b in range(BLOCKS)], axis=0
+            [x[:, b * F + CUTS[j] : b * F + CUTS[j + 1]] for b in range(BLOCKS)], axis=0
         )
         product = lax.dot_general(
             weights, samples, (((1,), (1,)), ((), ())), preferred_element_type=jnp.float32
@@ -114,9 +116,7 @@
         parts[KEEP * m + HALF : KEEP * (m + 1), :] = cosine - turned
 
     def put(channel, group, rows):
-        rows = rows.astype(jnp.bfloat16)
-        out_ref[channel, group] = rows
-        out_ref[KEEP + channel, group] = rows
+        out_ref[channel % ROW, channel // ROW, group] = rows
 
     for p in range(HALF):
         for a in range(GROUPS):
@@ -150,89 +150,128 @@
     return pl.pallas_call(
         channelize_kernel,
         in_specs=[anywhere] * 3,
-        out_shape=jax.ShapeDtypeStruct((2 * KEEP, GROUPS, BLOCKS, 128), jnp.bfloat16),
+        out_shape=jax.ShapeDtypeStruct((ROW, LINE, GROUPS, BLOCKS, 128), jnp.float32),
         scratch_shapes=[
             pltpu.VMEM((128, BLOCKS * F), jnp.bfloat16),
             pltpu.VMEM((TAPS, F), jnp.float32),
             pltpu.VMEM((40, F), jnp.float32),
             pltpu.VMEM((ROWS, BLOCKS * 128), jnp.float32),
             pltpu.VMEM((GROUPS * BLOCKS * KEEP, 128), jnp.float32),
-            pltpu.SemaphoreType.DMA((2 + STEPS * BLOCKS,)),
+            pltpu.SemaphoreType.DMA((STEPS, 2 + BLOCKS)),
         ],
         compiler_params=pltpu.CompilerParams(vmem_limit_bytes=40 * 1024 * 1024),
         name="channelize",
     )(samples, taps, table)
 
 
-def overlap_kernel(recv_ref, out_ref, wide):
-    row = lax.broadcasted_iota(jnp.int32, (BLOCKS, 128), 0)
+def row_kernel(recv_ref, out_ref, wide):
+    for g in range(SPAN // BLOCKS):
+        total = None
+        for y in range(ROW):
+            if 0 <= g - y < GROUPS:
+                share = recv_ref[y, :, g - y]
+                total = share if total is None else total + share
+        wide[:, BLOCKS * g : BLOCKS * (g + 1), :] = total
+    done = wide[...].astype(jnp.bfloat16)
+    out_ref[:LINE] = done
+    out_ref[LINE:] = done
+
+
+def add_row(recv):
+    recv = pltpu.with_memory_space_constraint(recv, pltpu.VMEM)
+    return pl.pallas_call(
+        row_kernel,
+        in_specs=[pl.BlockSpec(memory_space=pltpu.VMEM)],
+        out_specs=pl.BlockSpec(memory_space=pltpu.VMEM),
+        out_shape=pltpu.VMEM((2 * LINE, SPAN, 128), jnp.bfloat16),
+        scratch_shapes=[pltpu.VMEM((LINE, SPAN, 128), jnp.float32)],
+        name="add_row",
+    )(recv)
+
+
+def line_kernel(recv_ref, out_ref):
     for z in range(2):
-        for d in range(KEEP):
-            total = jnp.zeros((BLOCKS, 128), jnp.float32)
-            if BLOCKS * (d + 1) >= TAPS:
-                for a in range(min(d + 1, GROUPS)):
-                    total += recv_ref[KEEP * z + d - a, a].astype(jnp.float32)
-                if BLOCKS * d < TAPS - 1:
-                    total = jnp.where(BLOCKS * d + row >= TAPS - 1, total, 0.0)
-            at = KEEP * BLOCKS * z + BLOCKS * d
-            wide[at : at + BLOCKS, :] = total
-    done = wide[...].astype(jnp.bfloat16).reshape(2, BLOCKS * KEEP, 128)
-    for x in range(out_ref.shape[0]):
-        out_ref[x] = done
-
-
-def overlap(recv, copies):
-    return pl.pallas_call(
-        overlap_kernel,
-        out_shape=jax.ShapeDtypeStruct((copies, 2, BLOCKS * KEEP, 128), jnp.bfloat16),
-        scratch_shapes=[pltpu.VMEM((2 * BLOCKS * KEEP, 128), jnp.float32)],
-        name="overlap",
+        for d in range(LINE):
+            total = recv_ref[LINE * z + d, :TAPS].astype(jnp.float32)
+            if d:
+                total += recv_ref[LINE * z + d - 1, TAPS:].astype(jnp.float32)
+            else:
+                row = lax.broadcasted_iota(jnp.int32, total.shape, 0)
+                total = jnp.where(row == TAPS - 1, total, 0.0)
+            done = total.astype(jnp.bfloat16)
+            for x in range(out_ref.shape[0]):
+                out_ref[x, z, TAPS * d : TAPS * (d + 1), :] = done
+
+
+def add_line(recv, copies):
+    recv = pltpu.with_memory_space_constraint(recv, pltpu.VMEM)
+    return pl.pallas_call(
+        line_kernel,
+        in_specs=[pl.BlockSpec(memory_space=pltpu.VMEM)],
+        out_specs=pl.BlockSpec(memory_space=pltpu.VMEM),
+        out_shape=pltpu.VMEM((copies, 2, BLOCKS * KEEP, 128), jnp.bfloat16),
+        name="add_line",
     )(recv)
 
 
-def products_kernel(me_ref, all_ref, out_ref):
-    mine = all_ref[me_ref[0], me_ref[1]].astype(jnp.float32)
+def products_kernel(all_ref, out_hbm, done, sems):
+    own = 2 * lax.axis_index("x") + lax.axis_index("zh")
+    mine = all_ref[lax.axis_index("c"), own].astype(jnp.float32)
     lane = lax.broadcasted_iota(jnp.int32, mine.shape, 1)
-    turned = pltpu.roll(mine, 64, 1) * jnp.where(lane < 64, 1.0, -1.0)
-    left = jnp.concatenate([mine, turned], axis=0).astype(jnp.bfloat16)
     first = lane < 64
-    for pair in range(all_ref.shape[1]):
-        one = all_ref[0, pair].astype(jnp.float32)
-        two = all_ref[1, pair].astype(jnp.float32)
-        real = jnp.where(first, one, pltpu.roll(two, 64, 1))
-        imag = jnp.where(first, pltpu.roll(one, 64, 1), two)
-        right = jnp.concatenate([real, imag], axis=0).astype(jnp.bfloat16)
-        full = lax.dot_general(
-            left, right, (((0,), (0,)), ((), ())), preferred_element_type=jnp.float32
-        ) * (1.0 / NS)
-        out_ref[0, 0, :, 128 * pair : 128 * (pair + 1)] = full[:64]
-        out_ref[0, 1, :, 128 * pair : 128 * (pair + 1)] = full[64:]
-
-
-def products(me, everyone):
-    pairs = everyone.shape[1]
+    turned = pltpu.roll(mine, 64, 1) * jnp.where(first, 1.0, -1.0)
+    left = jnp.concatenate([mine.T, turned.T], axis=1).astype(jnp.bfloat16)
+    copies = []
+    for x in range(all_ref.shape[1] // 2):
+        real, imag = [], []
+        for pair in (2 * x, 2 * x + 1):
+            one = all_ref[0, pair].astype(jnp.float32)
+            two = all_ref[1, pair].astype(jnp.float32)
+            real.append(jnp.where(first, one, pltpu.roll(two, 64, 1)))
+            imag.append(jnp.where(first, pltpu.roll(one, 64, 1), two))
+        right = jnp.concatenate(
+            [jnp.concatenate(real, axis=1), jnp.concatenate(imag, axis=1)], axis=0
+        ).astype(jnp.bfloat16)
+        full = jnp.dot(left, right, preferred_element_type=jnp.float32) * (1.0 / NS)
+        here = slice(256 * x, 256 * (x + 1))
+        done[0, :, here] = full[:64]
+        done[1, :, here] = full[64:]
+        at = pl.ds(256 * x, 256)
+        copy = pltpu.make_async_copy(done.at[:, :, at], out_hbm.at[0, :, :, at], sems.at[x])
+        copy.start()
+        copies.append(copy)
+    for copy in copies:
+        copy.wait()
+
+
+def products(everyone):
+    inputs = 128 * everyone.shape[1]
+    everyone = pltpu.with_memory_space_constraint(everyone, pltpu.VMEM)
     return pl.pallas_call(
         products_kernel,
-        in_specs=[
-            pl.BlockSpec(memory_space=pltpu.SMEM),
-            pl.BlockSpec(memory_space=pltpu.VMEM),
+        in_specs=[pl.BlockSpec(memory_space=pltpu.VMEM)],
+        out_specs=pl.BlockSpec(memory_space=pltpu.HBM),
+        out_shape=jax.ShapeDtypeStruct((1, 2, 64, inputs), jnp.float32),
+        scratch_shapes=[
+            pltpu.VMEM((2, 64, inputs), jnp.float32),
+            pltpu.SemaphoreType.DMA((inputs // 256,)),
         ],
-        out_shape=jax.ShapeDtypeStruct((1, 2, 64, 128 * pairs), jnp.float32),
         name="products",
-    )(me, everyone)
+    )(everyone)
 
 
 def body(voltages):
     taps = jnp.asarray(make_taps())
     table = jnp.asarray(make_table())
     sent = channelize(voltages, taps, table)
-    recv = lax.all_to_all(sent, ("zh", "zl", "y"), split_axis=0, concat_axis=0, tiled=True)
-    mine = overlap(recv, 4)
+    recv = lax.all_to_all(sent, "y", split_axis=0, concat_axis=0, tiled=True)
+    line = add_row(recv)
+    recv = lax.all_to_all(line, ("zh", "zl"), split_axis=0, concat_axis=0, tiled=True)
+    mine = add_line(recv, 4)
     row = lax.all_to_all(mine, "x", split_axis=0, concat_axis=0, tiled=True)
     row = row.reshape(8, BLOCKS * KEEP, 128)
     everyone = lax.all_gather(row, "c", axis=0)
-    me = jnp.stack([lax.axis_index("c"), 2 * lax.axis_index("x") + lax.axis_index("zh")])
-    return products(me.astype(jnp.int32), everyone)
+    return products(everyone)
 
 
 def solution(mesh):

time: 68.1 us -> 61 us (0.90)
  blocking collectives: 48.5 us -> 54.1 us
  waiting for transfers between devices: 4.88 us -> 0 us
  starting transfers between devices: 4.17 us -> 0 us
  Pallas kernels: 9.62 us -> 6.71 us
    all_to_all x1 -> x3, blocking collectives: 41.3 us -> 47 us  [the longest x1 27 us: body(): lax.all_to_all(line, ('zh', 'zl'), split_axis=0, concat_axis=0, tiled=True)]
    all_to_all x1 -> x0, waiting for transfers between devices: 4.88 us -> none  [body(): row = lax.all_to_all(mine, 'x', split_axis=0, concat_axis=0, tiled=True)]
    all_to_all x1 -> x0, starting transfers between devices: 4.17 us -> none  [body(): row = lax.all_to_all(mine, 'x', split_axis=0, concat_axis=0, tiled=True)]
    pallas_call x1 -> x2, Pallas kernels: 1.77 us -> 0.07 us  [the longest x1 0.05 us: add_row(): pl.pallas_call(row_kernel, in_specs=[pl.BlockSpec(memory_space=pltpu.VMEM...]
    pallas_call x1, Pallas kernels: 2.29 us -> 1.26 us  [products(): pl.pallas_call(products_kernel, in_specs=[pl.BlockSpec(memory_space=pltpu...]
  transfers between devices with their start and end apart: 1 -> 0, of which waited for: 1 -> 0; matrix products, arithmetic and copies ran while one was open for 1% -> 0% of each run, Pallas kernels for 0% -> 0%
where the time goes in v3:
time: 61 us; the launch traced here: 60.8 us
  blocking collectives  54.1 us (89%)
  Pallas kernels  6.71 us (11%)
    all_to_all x1, blocking collectives, body(): lax.all_to_all(line, ('zh', 'zl'), split_axis=0, concat_axis=0, tiled=True)  27 us
    all_to_all x1, blocking collectives, body(): recv = lax.all_to_all(sent, 'y', split_axis=0, concat_axis=0, tiled=True)  10.7 us
    all_to_all x1, blocking collectives, body(): row = lax.all_to_all(mine, 'x', split_axis=0, concat_axis=0, tiled=True)  9.34 us
    all_gather x1, blocking collectives, body(): everyone = lax.all_gather(row, 'c', axis=0)  7.03 us
    pallas_call x1, Pallas kernels, channelize(): pl.pallas_call(channelize_kernel, in_specs=[anywhere] * 3, out_shape=jax....  5.38 us
    pallas_call x1, Pallas kernels, products(): pl.pallas_call(products_kernel, in_specs=[pl.BlockSpec(memory_space=pltpu...  1.26 us

profile of v3, /device:TPU:1, one launch (start us, length us, event | category | flops | bytes accessed | tf_op | source)
XLA Modules:
  0.0 60.8 jit_solution(13702798282693181686)
XLA Ops:
  0.0 5.4 %channelize.1 = f32[4,8,5,4,128]{4,3,2,1,0:T(4,128)S(1)} custom-call(bf16[128,16384]{1,0:T(8,128)(2,1)} %bitcast.2, f32[16,4096]{1,0:T(8,128)} %constant.4.clone.taps_hbm, f32[40,4096]{1,0:T(8,128)} %constant.5.clone.table_hbm), custom_call_target="tpu_custom_call" | custom-call | tf_op jit(solution)/shard_map/channelize/pallas_call | solution.py:150
  5.4 10.7 %all_to_all.15.recv_ref = f32[4,8,5,4,128]{4,3,2,1,0:T(4,128)S(1)} all-to-all(f32[4,8,5,4,128]{4,3,2,1,0:T(4,128)S(1)} %channelize.1), channel_id=1, replica_groups=mesh['zl'=8,'y'=4,'x'=4,'zh'=2,'c'=2] {'y'}, dimensions={0} | all-to-all | bytes 655360 | tf_op jit(solution)/shard_map/all_to_all | solution.py:267
  16.1 0.1 add_row.1
  16.1 27.0 %all_to_all.16.recv_ref = bf16[16,32,128]{2,1,0:T(8,128)(2,1)S(1)} all-to-all(bf16[16,32,128]{2,1,0:T(8,128)(2,1)S(1)} %add_row.1), channel_id=1, replica_groups=mesh['zl'=8,'y'=4,'x'=4,'zh'=2,'c'=2] {'zh','zl'}, dimensions={0} | all-to-all | bytes 262144 | tf_op jit(solution)/shard_map/all_to_all | solution.py:269
  43.2 9.3 %all_to_all.17 = bf16[4,2,128,128]{3,2,1,0:T(8,128)(2,1)S(1)} all-to-all(bf16[4,2,128,128]{3,2,1,0:T(8,128)(2,1)S(1)} %add_line.1), channel_id=1, replica_groups=mesh['zl'=8,'y'=4,'x'=4,'zh'=2,'c'=2] {'x'}, dimensions={0} | all-to-all | bytes 524288 | tf_op jit(solution)/shard_map/all_to_all | solution.py:271
  52.5 7.0 %all_gather.3.all_ref = bf16[2,8,128,128]{3,2,1,0:T(8,128)(2,1)S(1)} all-gather(bf16[1,8,128,128]{3,2,1,0:T(8,128)(2,1)S(1)} %bitcast.3), channel_id=1, replica_groups=mesh['zl'=8,'y'=4,'x'=4,'zh'=2,'c'=2] {'c'}, dimensions={0}, use_global_device_ids=true | all-gather | bytes 786432 | tf_op jit(solution)/shard_map/all_gather | solution.py:273
  59.5 1.3 %products.1 = f32[1,2,64,1024]{3,2,1,0:T(8,128)} custom-call(bf16[2,8,128,128]{3,2,1,0:T(8,128)(2,1)S(1)} %all_gather.3.all_ref), custom_call_target="tpu_custom_call" | custom-call | tf_op jit(solution)/shard_map/products/pallas_call | solution.py:250
  (1 shorter events, 0.0 us)

commit v4 on v3

--- a/solution.py
+++ b/solution.py
@@ -18,7 +18,7 @@
 ROW = 4
 LINE = KEEP // ROW
 SPAN = 32
-CUTS = (0, 512, 1536, 2816, 4096)
+CUTS = (0, 1024, 2560, 4096)
 STEPS = len(CUTS) - 1
 FINE = (7, 8)
 EDGE = KEEP * TAPS
@@ -63,7 +63,10 @@
         ]
         for b in range(BLOCKS):
             at = pl.ds(b * F + CUTS[j], size)
-            own.append(pltpu.make_async_copy(x_hbm.at[:, at], x.at[:, at], sems.at[j, 2 + b]))
+            copy = pltpu.make_async_copy(
+                x_hbm.at[:, at], x.at[128 * b : 128 * (b + 1), here], sems.at[j, 2 + b]
+            )
+            own.append(copy)
         for copy in own:
             copy.start()
         copies.append(own)
@@ -85,11 +88,8 @@
         weights = jnp.concatenate(main + [high] + fine + [low], axis=0)
         for copy in copies[j][2:]:
             copy.wait()
-        samples = jnp.concatenate(
-            [x[:, b * F + CUTS[j] : b * F + CUTS[j + 1]] for b in range(BLOCKS)], axis=0
-        )
         product = lax.dot_general(
-            weights, samples, (((1,), (1,)), ((), ())), preferred_element_type=jnp.float32
+            weights, x[:, here], (((1,), (1,)), ((), ())), preferred_element_type=jnp.float32
         )
         if j == 0:
             acc[...] = product
@@ -116,7 +116,7 @@
         parts[KEEP * m + HALF : KEEP * (m + 1), :] = cosine - turned
 
     def put(channel, group, rows):
-        out_ref[channel % ROW, channel // ROW, group] = rows
+        out_ref[channel % ROW, channel // ROW, group] = rows.astype(jnp.bfloat16)
 
     for p in range(HALF):
         for a in range(GROUPS):
@@ -150,9 +150,10 @@
     return pl.pallas_call(
         channelize_kernel,
         in_specs=[anywhere] * 3,
-        out_shape=jax.ShapeDtypeStruct((ROW, LINE, GROUPS, BLOCKS, 128), jnp.float32),
+        out_specs=pl.BlockSpec(memory_space=pltpu.VMEM),
+        out_shape=pltpu.VMEM((ROW, LINE, GROUPS, BLOCKS, 128), jnp.bfloat16),
         scratch_shapes=[
-            pltpu.VMEM((128, BLOCKS * F), jnp.bfloat16),
+            pltpu.VMEM((128 * BLOCKS, F), jnp.bfloat16),
             pltpu.VMEM((TAPS, F), jnp.float32),
             pltpu.VMEM((40, F), jnp.float32),
             pltpu.VMEM((ROWS, BLOCKS * 128), jnp.float32),
@@ -169,7 +170,7 @@
         total = None
         for y in range(ROW):
             if 0 <= g - y < GROUPS:
-                share = recv_ref[y, :, g - y]
+                share = recv_ref[y, :, g - y].astype(jnp.float32)
                 total = share if total is None else total + share
         wide[:, BLOCKS * g : BLOCKS * (g + 1), :] = total
     done = wide[...].astype(jnp.bfloat16)

time: 61 us -> 59.8 us (0.980)
  blocking collectives: 54.1 us -> 52.9 us
    all_to_all x1, blocking collectives: 10.7 us -> 9.81 us  [body(): recv = lax.all_to_all(sent, 'y', split_axis=0, concat_axis=0, tiled=True)]
where the time goes in v4:
time: 59.8 us; the launch traced here: 59.6 us
  blocking collectives  52.9 us (88%)
  Pallas kernels  6.67 us (11%)
    all_to_all x1, blocking collectives, body(): lax.all_to_all(line, ('zh', 'zl'), split_axis=0, concat_axis=0, tiled=True)  26.7 us
    all_to_all x1, blocking collectives, body(): recv = lax.all_to_all(sent, 'y', split_axis=0, concat_axis=0, tiled=True)  9.81 us
    all_to_all x1, blocking collectives, body(): row = lax.all_to_all(mine, 'x', split_axis=0, concat_axis=0, tiled=True)  9.35 us
    all_gather x1, blocking collectives, body(): everyone = lax.all_gather(row, 'c', axis=0)  7.05 us
    pallas_call x1, Pallas kernels, channelize(): pl.pallas_call(channelize_kernel, in_specs=[anywhere] * 3, out_specs=pl.B...  5.34 us
    pallas_call x1, Pallas kernels, products(): pl.pallas_call(products_kernel, in_specs=[pl.BlockSpec(memory_space=pltpu...  1.26 us

profile of v4, /device:TPU:1, one launch (start us, length us, event | category | flops | bytes accessed | tf_op | source)
XLA Modules:
  0.0 59.6 jit_solution(9046405314552241931)
XLA Ops:
  0.0 5.3 %channelize.1 = bf16[4,8,5,4,128]{4,3,2,1,0:T(4,128)(2,1)S(1)} custom-call(bf16[128,16384]{1,0:T(8,128)(2,1)} %bitcast.2, f32[16,4096]{1,0:T(8,128)} %constant.4.clone.taps_hbm, f32[40,4096]{1,0:T(8,128)} %constant.5.clone.table_hbm), custom_call_target="tpu_custom_call" | custom-call | tf_op jit(solution)/shard_map/channelize/pallas_call | solution.py:150
  5.3 9.8 %all_to_all.15.recv_ref = bf16[4,8,5,4,128]{4,3,2,1,0:T(4,128)(2,1)S(1)} all-to-all(bf16[4,8,5,4,128]{4,3,2,1,0:T(4,128)(2,1)S(1)} %channelize.1), channel_id=1, replica_groups=mesh['zl'=8,'y'=4,'x'=4,'zh'=2,'c'=2] {'y'}, dimensions={0} | all-to-all | bytes 327680 | tf_op jit(solution)/shard_map/all_to_all | solution.py:268
  15.2 0.1 add_row.1
  15.2 26.7 %all_to_all.16.recv_ref = bf16[16,32,128]{2,1,0:T(8,128)(2,1)S(1)} all-to-all(bf16[16,32,128]{2,1,0:T(8,128)(2,1)S(1)} %add_row.1), channel_id=1, replica_groups=mesh['zl'=8,'y'=4,'x'=4,'zh'=2,'c'=2] {'zh','zl'}, dimensions={0} | all-to-all | bytes 262144 | tf_op jit(solution)/shard_map/all_to_all | solution.py:270
  42.0 9.3 %all_to_all.17 = bf16[4,2,128,128]{3,2,1,0:T(8,128)(2,1)S(1)} all-to-all(bf16[4,2,128,128]{3,2,1,0:T(8,128)(2,1)S(1)} %add_line.1), channel_id=1, replica_groups=mesh['zl'=8,'y'=4,'x'=4,'zh'=2,'c'=2] {'x'}, dimensions={0} | all-to-all | bytes 524288 | tf_op jit(solution)/shard_map/all_to_all | solution.py:272
  51.3 7.0 %all_gather.3.all_ref = bf16[2,8,128,128]{3,2,1,0:T(8,128)(2,1)S(1)} all-gather(bf16[1,8,128,128]{3,2,1,0:T(8,128)(2,1)S(1)} %bitcast.3), channel_id=1, replica_groups=mesh['zl'=8,'y'=4,'x'=4,'zh'=2,'c'=2] {'c'}, dimensions={0}, use_global_device_ids=true | all-gather | bytes 786432 | tf_op jit(solution)/shard_map/all_gather | solution.py:274
  58.4 1.3 %products.1 = f32[1,2,64,1024]{3,2,1,0:T(8,128)} custom-call(bf16[2,8,128,128]{3,2,1,0:T(8,128)(2,1)S(1)} %all_gather.3.all_ref), custom_call_target="tpu_custom_call" | custom-call | tf_op jit(solution)/shard_map/products/pallas_call | solution.py:251
  (1 shorter events, 0.0 us)

commit v5 on v4

--- a/solution.py
+++ b/solution.py
@@ -17,14 +17,15 @@
 GROUPS = 5
 ROW = 4
 LINE = KEEP // ROW
+TABLE = 40
 SPAN = 32
 CUTS = (0, 1024, 2560, 4096)
 STEPS = len(CUTS) - 1
 FINE = (7, 8)
 EDGE = KEEP * TAPS
-FINES = EDGE + KEEP
+FINES = EDGE + TAPS
 FINE_EDGE = FINES + KEEP * len(FINE)
-ROWS = FINE_EDGE + KEEP
+ROWS = FINE_EDGE + TAPS
 
 
 def make_taps():
@@ -42,7 +43,7 @@
     turns = (MIDDLE + np.arange(HALF + 1))[:, None] * np.arange(F)[None, :] % F
     phase = 2.0 * np.pi * turns / F
     cosine, sine = np.cos(phase) * F**-0.5, np.sin(phase) * F**-0.5
-    rows = [cosine[:HALF], sine[:HALF], cosine[HALF:], sine[HALF:], np.zeros((6, F))]
+    rows = [cosine[:HALF], cosine[HALF:], sine[1:], np.zeros((TABLE - KEEP - 1, F))]
     table = np.concatenate(rows, axis=0).astype(np.float32)
     return table.astype(jnp.bfloat16).astype(np.float32)
 
@@ -52,19 +53,18 @@
     return high, (weight - high.astype(jnp.float32)).astype(jnp.bfloat16)
 
 
-def channelize_kernel(x_hbm, taps_hbm, table_hbm, out_ref, x, taps, table, acc, parts, sems):
+def channelize_kernel(x_hbm, table_hbm, out_ref, x, table, acc, parts, sems):
     copies = []
     for j in range(STEPS):
         size = CUTS[j + 1] - CUTS[j]
         here = pl.ds(CUTS[j], size)
         own = [
-            pltpu.make_async_copy(taps_hbm.at[:, here], taps.at[:, here], sems.at[j, 0]),
-            pltpu.make_async_copy(table_hbm.at[:, here], table.at[:, here], sems.at[j, 1]),
+            pltpu.make_async_copy(table_hbm.at[:, here], table.at[:, here], sems.at[j, 0]),
         ]
         for b in range(BLOCKS):
             at = pl.ds(b * F + CUTS[j], size)
             copy = pltpu.make_async_copy(
-                x_hbm.at[:, at], x.at[128 * b : 128 * (b + 1), here], sems.at[j, 2 + b]
+                x_hbm.at[:, at], x.at[128 * b : 128 * (b + 1), here], sems.at[j, 1 + b]
             )
             own.append(copy)
         for copy in own:
@@ -73,20 +73,19 @@
 
     for j in range(STEPS):
         here = slice(CUTS[j], CUTS[j + 1])
-        for copy in copies[j][:2]:
+        for copy in copies[j][:1]:
             copy.wait()
-        tap = taps[:, here]
-        wide = table[:, here]
+        tap = table[:TAPS, here]
+        wide = table[TAPS:, here]
         main, fine = [], []
         for i in range(TAPS):
             high, low = split(wide[:KEEP] * tap[i : i + 1])
             main.append(high)
             if i in FINE:
                 fine.append(low)
-        edge = jnp.concatenate([tap * wide[KEEP : KEEP + 1], tap * wide[KEEP + 1 : KEEP + 2]], axis=0)
-        high, low = split(edge)
+        high, low = split(tap * wide[KEEP : KEEP + 1])
         weights = jnp.concatenate(main + [high] + fine + [low], axis=0)
-        for copy in copies[j][2:]:
+        for copy in copies[j][1:]:
             copy.wait()
         product = lax.dot_general(
             weights, x[:, here], (((1,), (1,)), ((), ())), preferred_element_type=jnp.float32
@@ -98,6 +97,7 @@
 
     lane = lax.broadcasted_iota(jnp.int32, (1, 128), 1)
     sign = jnp.where(lane < 64, 1.0, -1.0).astype(jnp.float32)
+    row = lax.broadcasted_iota(jnp.int32, (HALF, 128), 0)
     for m in range(GROUPS * BLOCKS):
         cosine = jnp.zeros((HALF, 128), jnp.float32)
         sine = jnp.zeros((HALF, 128), jnp.float32)
@@ -108,61 +108,56 @@
             rows = [KEEP * i]
             if i in FINE:
                 rows.append(FINES + KEEP * FINE.index(i))
-            for row in rows:
-                cosine += acc[row : row + HALF, 128 * b : 128 * (b + 1)]
-                sine += acc[row + HALF : row + KEEP, 128 * b : 128 * (b + 1)]
-        turned = sign * pltpu.roll(sine, 64, 1)
+            for at in rows:
+                cosine += acc[at : at + HALF, 128 * b : 128 * (b + 1)]
+                sine += acc[at + HALF : at + KEEP, 128 * b : 128 * (b + 1)]
+        turned = jnp.where(row == 0, 0.0, sign * pltpu.roll(sine, 64, 1))
         parts[KEEP * m : KEEP * m + HALF, :] = cosine + turned
-        parts[KEEP * m + HALF : KEEP * (m + 1), :] = cosine - turned
+        parts[KEEP * m + HALF : KEEP * (m + 1), :] = jnp.where(row == 0, sine, cosine - turned)
 
     def put(channel, group, rows):
         out_ref[channel % ROW, channel // ROW, group] = rows.astype(jnp.bfloat16)
 
+    edge = acc[EDGE:FINES, :] + acc[FINE_EDGE:ROWS, :]
+    total = jnp.zeros((GROUPS * BLOCKS, 128), jnp.float32)
+    for b in range(BLOCKS):
+        pieces = [edge[:, 128 * b : 128 * (b + 1)], jnp.zeros((BLOCKS - b, 128), jnp.float32)]
+        if b:
+            pieces.insert(0, jnp.zeros((b, 128), jnp.float32))
+        total += jnp.concatenate(pieces, axis=0)
+    total = sign * pltpu.roll(total, 64, 1)
     for p in range(HALF):
         for a in range(GROUPS):
             above = parts[pl.ds(KEEP * BLOCKS * a + p, BLOCKS, stride=KEEP), :]
             put(HALF + p, a, above)
+            below = parts[pl.ds(KEEP * BLOCKS * a + HALF + p, BLOCKS, stride=KEEP), :]
             if p:
-                below = parts[pl.ds(KEEP * BLOCKS * a + HALF + p, BLOCKS, stride=KEEP), :]
                 put(HALF - p, a, below)
-    edge = acc[EDGE:FINES, :] + acc[FINE_EDGE:ROWS, :]
-    total = jnp.zeros((GROUPS * BLOCKS, 128), jnp.float32)
-    for b in range(BLOCKS):
-        cosine = edge[:TAPS, 128 * b : 128 * (b + 1)]
-        sine = edge[TAPS:, 128 * b : 128 * (b + 1)]
-        share = cosine - sign * pltpu.roll(sine, 64, 1)
-        pieces = [share]
-        if b:
-            pieces.insert(0, jnp.zeros((b, 128), jnp.float32))
-        if b < BLOCKS:
-            pieces.append(jnp.zeros((BLOCKS - b, 128), jnp.float32))
-        total += jnp.concatenate(pieces, axis=0)
-    for a in range(GROUPS):
-        put(0, a, total[BLOCKS * a : BLOCKS * (a + 1)])
-
-
-def channelize(voltages, taps, table):
+            else:
+                put(0, a, below - total[BLOCKS * a : BLOCKS * (a + 1)])
+
+
+def channelize(voltages, table):
     samples = voltages.reshape(128, BLOCKS * F)
-    samples, taps, table = (
-        pltpu.with_memory_space_constraint(array, pltpu.HBM) for array in (samples, taps, table)
+    samples, table = (
+        pltpu.with_memory_space_constraint(array, pltpu.HBM) for array in (samples, table)
     )
     anywhere = pl.BlockSpec(memory_space=pltpu.HBM)
     return pl.pallas_call(
         channelize_kernel,
-        in_specs=[anywhere] * 3,
+        in_specs=[anywhere] * 2,
         out_specs=pl.BlockSpec(memory_space=pltpu.VMEM),
         out_shape=pltpu.VMEM((ROW, LINE, GROUPS, BLOCKS, 128), jnp.bfloat16),
         scratch_shapes=[
             pltpu.VMEM((128 * BLOCKS, F), jnp.bfloat16),
-            pltpu.VMEM((TAPS, F), jnp.float32),
-            pltpu.VMEM((40, F), jnp.float32),
+            pltpu.VMEM((TAPS + TABLE, F), jnp.float32),
             pltpu.VMEM((ROWS, BLOCKS * 128), jnp.float32),
             pltpu.VMEM((GROUPS * BLOCKS * KEEP, 128), jnp.float32),
-            pltpu.SemaphoreType.DMA((STEPS, 2 + BLOCKS)),
+            pltpu.SemaphoreType.DMA((STEPS, 1 + BLOCKS)),
         ],
         compiler_params=pltpu.CompilerParams(vmem_limit_bytes=40 * 1024 * 1024),
         name="channelize",
-    )(samples, taps, table)
+    )(samples, table)
 
 
 def row_kernel(recv_ref, out_ref, wide):
@@ -262,9 +257,8 @@
 
 
 def body(voltages):
-    taps = jnp.asarray(make_taps())
-    table = jnp.asarray(make_table())
-    sent = channelize(voltages, taps, table)
+    table = jnp.asarray(np.concatenate([make_taps(), make_table()], axis=0))
+    sent = channelize(voltages, table)
     recv = lax.all_to_all(sent, "y", split_axis=0, concat_axis=0, tiled=True)
     line = add_row(recv)
     recv = lax.all_to_all(line, ("zh", "zl"), split_axis=0, concat_axis=0, tiled=True)

time: 59.8 us -> 59.6 us (level)
  no operation moved by 1% of the time
where the time goes in v5:
time: 59.6 us; the launch traced here: 59.4 us
  blocking collectives  52.9 us (89%)
  Pallas kernels  6.49 us (11%)
    all_to_all x1, blocking collectives, body(): lax.all_to_all(line, ('zh', 'zl'), split_axis=0, concat_axis=0, tiled=True)  26.7 us
    all_to_all x1, blocking collectives, body(): recv = lax.all_to_all(sent, 'y', split_axis=0, concat_axis=0, tiled=True)  9.81 us
    all_to_all x1, blocking collectives, body(): row = lax.all_to_all(mine, 'x', split_axis=0, concat_axis=0, tiled=True)  9.34 us
    all_gather x1, blocking collectives, body(): everyone = lax.all_gather(row, 'c', axis=0)  7.05 us
    pallas_call x1, Pallas kernels, channelize(): pl.pallas_call(channelize_kernel, in_specs=[anywhere] * 2, out_specs=pl.B...  5.15 us
    pallas_call x1, Pallas kernels, products(): pl.pallas_call(products_kernel, in_specs=[pl.BlockSpec(memory_space=pltpu...  1.26 us

profile of v5, /device:TPU:1, one launch (start us, length us, event | category | flops | bytes accessed | tf_op | source)
XLA Modules:
  0.0 59.4 jit_solution(8232261203860622537)
XLA Ops:
  0.0 5.2 %channelize.1 = bf16[4,8,5,4,128]{4,3,2,1,0:T(4,128)(2,1)S(1)} custom-call(bf16[128,16384]{1,0:T(8,128)(2,1)} %bitcast.2, f32[56,4096]{1,0:T(8,128)} %constant.2.clone.table_hbm), custom_call_target="tpu_custom_call" | custom-call | tf_op jit(solution)/shard_map/channelize/pallas_call | solution.py:146
  5.2 9.8 %all_to_all.15.recv_ref = bf16[4,8,5,4,128]{4,3,2,1,0:T(4,128)(2,1)S(1)} all-to-all(bf16[4,8,5,4,128]{4,3,2,1,0:T(4,128)(2,1)S(1)} %channelize.1), channel_id=1, replica_groups=mesh['zl'=8,'y'=4,'x'=4,'zh'=2,'c'=2] {'y'}, dimensions={0} | all-to-all | bytes 327680 | tf_op jit(solution)/shard_map/all_to_all | solution.py:262
  15.0 0.1 add_row.1
  15.0 26.7 %all_to_all.16.recv_ref = bf16[16,32,128]{2,1,0:T(8,128)(2,1)S(1)} all-to-all(bf16[16,32,128]{2,1,0:T(8,128)(2,1)S(1)} %add_row.1), channel_id=1, replica_groups=mesh['zl'=8,'y'=4,'x'=4,'zh'=2,'c'=2] {'zh','zl'}, dimensions={0} | all-to-all | bytes 262144 | tf_op jit(solution)/shard_map/all_to_all | solution.py:264
  41.8 9.3 %all_to_all.17 = bf16[4,2,128,128]{3,2,1,0:T(8,128)(2,1)S(1)} all-to-all(bf16[4,2,128,128]{3,2,1,0:T(8,128)(2,1)S(1)} %add_line.1), channel_id=1, replica_groups=mesh['zl'=8,'y'=4,'x'=4,'zh'=2,'c'=2] {'x'}, dimensions={0} | all-to-all | bytes 524288 | tf_op jit(solution)/shard_map/all_to_all | solution.py:266
  51.1 7.1 %all_gather.3.all_ref = bf16[2,8,128,128]{3,2,1,0:T(8,128)(2,1)S(1)} all-gather(bf16[1,8,128,128]{3,2,1,0:T(8,128)(2,1)S(1)} %bitcast.3), channel_id=1, replica_groups=mesh['zl'=8,'y'=4,'x'=4,'zh'=2,'c'=2] {'c'}, dimensions={0}, use_global_device_ids=true | all-gather | bytes 786432 | tf_op jit(solution)/shard_map/all_gather | solution.py:268
  58.2 1.3 %products.1 = f32[1,2,64,1024]{3,2,1,0:T(8,128)} custom-call(bf16[2,8,128,128]{3,2,1,0:T(8,128)(2,1)S(1)} %all_gather.3.all_ref), custom_call_target="tpu_custom_call" | custom-call | tf_op jit(solution)/shard_map/products/pallas_call | solution.py:246
  (1 shorter events, 0.0 us)

commit v6 on v5

--- a/solution.py
+++ b/solution.py
@@ -212,6 +212,7 @@
 
 def products_kernel(all_ref, out_hbm, done, sems):
     own = 2 * lax.axis_index("x") + lax.axis_index("zh")
+    turn = (lax.axis_index("x") // 2 + lax.axis_index("zh")) % 2
     mine = all_ref[lax.axis_index("c"), own].astype(jnp.float32)
     lane = lax.broadcasted_iota(jnp.int32, mine.shape, 1)
     first = lane < 64
@@ -221,8 +222,9 @@
     for x in range(all_ref.shape[1] // 2):
         real, imag = [], []
         for pair in (2 * x, 2 * x + 1):
-            one = all_ref[0, pair].astype(jnp.float32)
-            two = all_ref[1, pair].astype(jnp.float32)
+            core = turn if (x // 2 + pair) % 2 == 0 else 1 - turn
+            one = all_ref[core, pair].astype(jnp.float32)
+            two = all_ref[1 - core, pair].astype(jnp.float32)
             real.append(jnp.where(first, one, pltpu.roll(two, 64, 1)))
             imag.append(jnp.where(first, pltpu.roll(one, 64, 1), two))
         right = jnp.concatenate(
@@ -261,9 +263,15 @@
     sent = channelize(voltages, table)
     recv = lax.all_to_all(sent, "y", split_axis=0, concat_axis=0, tiled=True)
     line = add_row(recv)
-    recv = lax.all_to_all(line, ("zh", "zl"), split_axis=0, concat_axis=0, tiled=True)
+    groups = [[2 * z + (core ^ z // LINE) for z in range(2 * LINE)] for core in range(2)]
+    recv = lax.all_to_all(
+        line, ("zh", "zl", "c"), split_axis=0, concat_axis=0, axis_index_groups=groups, tiled=True
+    )
     mine = add_line(recv, 4)
-    row = lax.all_to_all(mine, "x", split_axis=0, concat_axis=0, tiled=True)
+    groups = [[2 * x + (core ^ x // 2) for x in range(4)] for core in range(2)]
+    row = lax.all_to_all(
+        mine, ("x", "c"), split_axis=0, concat_axis=0, axis_index_groups=groups, tiled=True
+    )
     row = row.reshape(8, BLOCKS * KEEP, 128)
     everyone = lax.all_gather(row, "c", axis=0)
     return products(everyone)

time: 59.6 us -> 58.6 us (0.983)
  blocking collectives: 52.9 us -> 51.9 us
    all_gather x1, blocking collectives: 7.05 us -> 3.63 us  [body(): everyone = lax.all_gather(row, 'c', axis=0)]
    all_to_all x2, blocking collectives: 36.1 us -> 38.4 us  [the longest x1 29.7 us: body(): lax.all_to_all(line, ('zh', 'zl', 'c'), split_axis=0, concat_axis=0, axis...]
where the time goes in v6:
time: 58.6 us; the launch traced here: 58.4 us
  blocking collectives  51.9 us (89%)
  Pallas kernels  6.48 us (11%)
    all_to_all x1, blocking collectives, body(): lax.all_to_all(line, ('zh', 'zl', 'c'), split_axis=0, concat_axis=0, axis...  29.7 us
    all_to_all x1, blocking collectives, body(): recv = lax.all_to_all(sent, 'y', split_axis=0, concat_axis=0, tiled=True)  9.81 us
    all_to_all x1, blocking collectives, body(): lax.all_to_all(mine, ('x', 'c'), split_axis=0, concat_axis=0, axis_index_...  8.75 us
    pallas_call x1, Pallas kernels, channelize(): pl.pallas_call(channelize_kernel, in_specs=[anywhere] * 2, out_specs=pl.B...  5.15 us
    all_gather x1, blocking collectives, body(): everyone = lax.all_gather(row, 'c', axis=0)  3.63 us
    pallas_call x1, Pallas kernels, products(): pl.pallas_call(products_kernel, in_specs=[pl.BlockSpec(memory_space=pltpu...  1.25 us

profile of v6, /device:TPU:1, one launch (start us, length us, event | category | flops | bytes accessed | tf_op | source)
XLA Modules:
  0.0 58.4 jit_solution(8704720751224075367)
XLA Ops:
  0.0 5.2 %channelize.1 = bf16[4,8,5,4,128]{4,3,2,1,0:T(4,128)(2,1)S(1)} custom-call(bf16[128,16384]{1,0:T(8,128)(2,1)} %bitcast.2, f32[56,4096]{1,0:T(8,128)} %constant.2.clone.table_hbm), custom_call_target="tpu_custom_call" | custom-call | tf_op jit(solution)/shard_map/channelize/pallas_call | solution.py:146
  5.2 9.8 %all_to_all.15.recv_ref = bf16[4,8,5,4,128]{4,3,2,1,0:T(4,128)(2,1)S(1)} all-to-all(bf16[4,8,5,4,128]{4,3,2,1,0:T(4,128)(2,1)S(1)} %channelize.1), channel_id=1, replica_groups=mesh['zl'=8,'y'=4,'x'=4,'zh'=2,'c'=2] {'y'}, dimensions={0} | all-to-all | bytes 327680 | tf_op jit(solution)/shard_map/all_to_all | solution.py:264
  15.0 0.1 add_row.1
  15.0 29.7 %all_to_all.16.recv_ref = bf16[16,32,128]{2,1,0:T(8,128)(2,1)S(1)} all-to-all(bf16[16,32,128]{2,1,0:T(8,128)(2,1)S(1)} %add_row.1), channel_id=1, replica_groups={{0,64,128,192,256,320,384,448,3,67,131,195,259,323,387,451},{1,65,129,1..., dimensions={0} | all-to-all | bytes 262144 | tf_op jit(solution)/shard_map/all_to_all | solution.py:267
  44.8 8.7 %all_to_all.17 = bf16[4,2,128,128]{3,2,1,0:T(8,128)(2,1)S(1)} all-to-all(bf16[4,2,128,128]{3,2,1,0:T(8,128)(2,1)S(1)} %add_line.1), channel_id=1, replica_groups={{0,4,9,13},{1,5,8,12},{2,6,11,15},{3,7,10,14},{16,20,25,29},{17,21,24,2..., dimensions={0} | all-to-all | bytes 524288 | tf_op jit(solution)/shard_map/all_to_all | solution.py:272
  53.5 3.6 %all_gather.3.all_ref = bf16[2,8,128,128]{3,2,1,0:T(8,128)(2,1)S(1)} all-gather(bf16[1,8,128,128]{3,2,1,0:T(8,128)(2,1)S(1)} %bitcast.3), channel_id=1, replica_groups=mesh['zl'=8,'y'=4,'x'=4,'zh'=2,'c'=2] {'c'}, dimensions={0}, use_global_device_ids=true | all-gather | bytes 786432 | tf_op jit(solution)/shard_map/all_gather | solution.py:276
  57.1 1.3 %products.1 = f32[1,2,64,1024]{3,2,1,0:T(8,128)} custom-call(bf16[2,8,128,128]{3,2,1,0:T(8,128)(2,1)S(1)} %all_gather.3.all_ref), custom_call_target="tpu_custom_call" | custom-call | tf_op jit(solution)/shard_map/products/pallas_call | solution.py:248
  (1 shorter events, 0.0 us)

commit v7 on v6

--- a/solution.py
+++ b/solution.py
@@ -18,6 +18,8 @@
 ROW = 4
 LINE = KEEP // ROW
 TABLE = 40
+Z_ORDER = tuple(5 * at % 16 for at in range(16))
+RING = (0, 2, 1, 3)
 SPAN = 32
 CUTS = (0, 1024, 2560, 4096)
 STEPS = len(CUTS) - 1
@@ -169,8 +171,8 @@
                 total = share if total is None else total + share
         wide[:, BLOCKS * g : BLOCKS * (g + 1), :] = total
     done = wide[...].astype(jnp.bfloat16)
-    out_ref[:LINE] = done
-    out_ref[LINE:] = done
+    for at, z in enumerate(Z_ORDER):
+        out_ref[at] = done[z % LINE]
 
 
 def add_row(recv):
@@ -188,9 +190,9 @@
 def line_kernel(recv_ref, out_ref):
     for z in range(2):
         for d in range(LINE):
-            total = recv_ref[LINE * z + d, :TAPS].astype(jnp.float32)
+            total = recv_ref[Z_ORDER.index(LINE * z + d), :TAPS].astype(jnp.float32)
             if d:
-                total += recv_ref[LINE * z + d - 1, TAPS:].astype(jnp.float32)
+                total += recv_ref[Z_ORDER.index(LINE * z + d - 1), TAPS:].astype(jnp.float32)
             else:
                 row = lax.broadcasted_iota(jnp.int32, total.shape, 0)
                 total = jnp.where(row == TAPS - 1, total, 0.0)
@@ -211,7 +213,9 @@
 
 
 def products_kernel(all_ref, out_hbm, done, sems):
-    own = 2 * lax.axis_index("x") + lax.axis_index("zh")
+    place = lax.axis_index("x")
+    place = 2 * (place % 2) + place // 2
+    own = 2 * place + lax.axis_index("zh")
     turn = (lax.axis_index("x") // 2 + lax.axis_index("zh")) % 2
     mine = all_ref[lax.axis_index("c"), own].astype(jnp.float32)
     lane = lax.broadcasted_iota(jnp.int32, mine.shape, 1)
@@ -222,9 +226,10 @@
     for x in range(all_ref.shape[1] // 2):
         real, imag = [], []
         for pair in (2 * x, 2 * x + 1):
+            came = 2 * RING[x] + pair % 2
             core = turn if (x // 2 + pair) % 2 == 0 else 1 - turn
-            one = all_ref[core, pair].astype(jnp.float32)
-            two = all_ref[1 - core, pair].astype(jnp.float32)
+            one = all_ref[core, came].astype(jnp.float32)
+            two = all_ref[1 - core, came].astype(jnp.float32)
             real.append(jnp.where(first, one, pltpu.roll(two, 64, 1)))
             imag.append(jnp.where(first, pltpu.roll(one, 64, 1), two))
         right = jnp.concatenate(
@@ -263,12 +268,12 @@
     sent = channelize(voltages, table)
     recv = lax.all_to_all(sent, "y", split_axis=0, concat_axis=0, tiled=True)
     line = add_row(recv)
-    groups = [[2 * z + (core ^ z // LINE) for z in range(2 * LINE)] for core in range(2)]
+    groups = [[2 * z + (core ^ z // LINE) for z in Z_ORDER] for core in range(2)]
     recv = lax.all_to_all(
         line, ("zh", "zl", "c"), split_axis=0, concat_axis=0, axis_index_groups=groups, tiled=True
     )
     mine = add_line(recv, 4)
-    groups = [[2 * x + (core ^ x // 2) for x in range(4)] for core in range(2)]
+    groups = [[2 * x + (core ^ x // 2) for x in RING] for core in range(2)]
     row = lax.all_to_all(
         mine, ("x", "c"), split_axis=0, concat_axis=0, axis_index_groups=groups, tiled=True
     )

time: 58.6 us -> 58 us (0.990)
  blocking collectives: 51.9 us -> 51.3 us
where the time goes in v7:
time: 58 us; the launch traced here: 57.8 us
  blocking collectives  51.3 us (88%)
  Pallas kernels  6.45 us (11%)
    all_to_all x1, blocking collectives, body(): lax.all_to_all(line, ('zh', 'zl', 'c'), split_axis=0, concat_axis=0, axis...  29.4 us
    all_to_all x1, blocking collectives, body(): recv = lax.all_to_all(sent, 'y', split_axis=0, concat_axis=0, tiled=True)  9.81 us
    all_to_all x1, blocking collectives, body(): lax.all_to_all(mine, ('x', 'c'), split_axis=0, concat_axis=0, axis_index_...  8.53 us
    pallas_call x1, Pallas kernels, channelize(): pl.pallas_call(channelize_kernel, in_specs=[anywhere] * 2, out_specs=pl.B...  5.15 us
    all_gather x1, blocking collectives, body(): everyone = lax.all_gather(row, 'c', axis=0)  3.56 us
    pallas_call x1, Pallas kernels, products(): pl.pallas_call(products_kernel, in_specs=[pl.BlockSpec(memory_space=pltpu...  1.22 us

profile of v7, /device:TPU:1, one launch (start us, length us, event | category | flops | bytes accessed | tf_op | source)
XLA Modules:
  0.0 57.8 jit_solution(5268057427633573265)
XLA Ops:
  0.0 5.2 %channelize.1 = bf16[4,8,5,4,128]{4,3,2,1,0:T(4,128)(2,1)S(1)} custom-call(bf16[128,16384]{1,0:T(8,128)(2,1)} %bitcast.2, f32[56,4096]{1,0:T(8,128)} %constant.2.clone.table_hbm), custom_call_target="tpu_custom_call" | custom-call | tf_op jit(solution)/shard_map/channelize/pallas_call | solution.py:148
  5.2 9.8 %all_to_all.15.recv_ref = bf16[4,8,5,4,128]{4,3,2,1,0:T(4,128)(2,1)S(1)} all-to-all(bf16[4,8,5,4,128]{4,3,2,1,0:T(4,128)(2,1)S(1)} %channelize.1), channel_id=1, replica_groups=mesh['zl'=8,'y'=4,'x'=4,'zh'=2,'c'=2] {'y'}, dimensions={0} | all-to-all | bytes 327680 | tf_op jit(solution)/shard_map/all_to_all | solution.py:269
  15.0 0.1 add_row.1
  15.0 29.4 %all_to_all.16.recv_ref = bf16[16,32,128]{2,1,0:T(8,128)(2,1)S(1)} all-to-all(bf16[16,32,128]{2,1,0:T(8,128)(2,1)S(1)} %add_row.1), channel_id=1, replica_groups={{0,320,131,451,256,67,387,192,3,323,128,448,259,64,384,195},{1,321,130,..., dimensions={0} | all-to-all | bytes 262144 | tf_op jit(solution)/shard_map/all_to_all | solution.py:272
  44.5 8.5 %all_to_all.17 = bf16[4,2,128,128]{3,2,1,0:T(8,128)(2,1)S(1)} all-to-all(bf16[4,2,128,128]{3,2,1,0:T(8,128)(2,1)S(1)} %add_line.1), channel_id=1, replica_groups={{0,9,4,13},{1,8,5,12},{2,11,6,15},{3,10,7,14},{16,25,20,29},{17,24,21,2..., dimensions={0} | all-to-all | bytes 524288 | tf_op jit(solution)/shard_map/all_to_all | solution.py:277
  53.0 3.6 %all_gather.3.all_ref = bf16[2,8,128,128]{3,2,1,0:T(8,128)(2,1)S(1)} all-gather(bf16[1,8,128,128]{3,2,1,0:T(8,128)(2,1)S(1)} %bitcast.3), channel_id=1, replica_groups=mesh['zl'=8,'y'=4,'x'=4,'zh'=2,'c'=2] {'c'}, dimensions={0}, use_global_device_ids=true | all-gather | bytes 786432 | tf_op jit(solution)/shard_map/all_gather | solution.py:281
  56.6 1.2 %products.1 = f32[1,2,64,1024]{3,2,1,0:T(8,128)} custom-call(bf16[2,8,128,128]{3,2,1,0:T(8,128)(2,1)S(1)} %all_gather.3.all_ref), custom_call_target="tpu_custom_call" | custom-call | tf_op jit(solution)/shard_map/products/pallas_call | solution.py:253
  (1 shorter events, 0.0 us)

commit v8 on v7

--- a/solution.py
+++ b/solution.py
@@ -18,7 +18,7 @@
 ROW = 4
 LINE = KEEP // ROW
 TABLE = 40
-Z_ORDER = tuple(5 * at % 16 for at in range(16))
+Z_ORDER = tuple(3 * at % 16 for at in range(16))
 RING = (0, 2, 1, 3)
 SPAN = 32
 CUTS = (0, 1024, 2560, 4096)
@@ -118,7 +118,7 @@
         parts[KEEP * m + HALF : KEEP * (m + 1), :] = jnp.where(row == 0, sine, cosine - turned)
 
     def put(channel, group, rows):
-        out_ref[channel % ROW, channel // ROW, group] = rows.astype(jnp.bfloat16)
+        out_ref[RING[channel % ROW], channel // ROW, group] = rows.astype(jnp.bfloat16)
 
     edge = acc[EDGE:FINES, :] + acc[FINE_EDGE:ROWS, :]
     total = jnp.zeros((GROUPS * BLOCKS, 128), jnp.float32)
@@ -167,7 +167,7 @@
         total = None
         for y in range(ROW):
             if 0 <= g - y < GROUPS:
-                share = recv_ref[y, :, g - y].astype(jnp.float32)
+                share = recv_ref[RING[y], :, g - y].astype(jnp.float32)
                 total = share if total is None else total + share
         wide[:, BLOCKS * g : BLOCKS * (g + 1), :] = total
     done = wide[...].astype(jnp.bfloat16)
@@ -266,7 +266,9 @@
 def body(voltages):
     table = jnp.asarray(np.concatenate([make_taps(), make_table()], axis=0))
     sent = channelize(voltages, table)
-    recv = lax.all_to_all(sent, "y", split_axis=0, concat_axis=0, tiled=True)
+    recv = lax.all_to_all(
+        sent, "y", split_axis=0, concat_axis=0, axis_index_groups=[list(RING)], tiled=True
+    )
     line = add_row(recv)
     groups = [[2 * z + (core ^ z // LINE) for z in Z_ORDER] for core in range(2)]
     recv = lax.all_to_all(

time: 58 us -> 57.7 us (level)
  no operation moved by 1% of the time
where the time goes in v8:
time: 57.7 us; the launch traced here: 57.5 us
  blocking collectives  51 us (88%)
  Pallas kernels  6.45 us (11%)
    all_to_all x1, blocking collectives, body(): lax.all_to_all(line, ('zh', 'zl', 'c'), split_axis=0, concat_axis=0, axis...  29.2 us
    all_to_all x1, blocking collectives, body(): lax.all_to_all(sent, 'y', split_axis=0, concat_axis=0, axis_index_groups=...  9.73 us
    all_to_all x1, blocking collectives, body(): lax.all_to_all(mine, ('x', 'c'), split_axis=0, concat_axis=0, axis_index_...  8.53 us
    pallas_call x1, Pallas kernels, channelize(): pl.pallas_call(channelize_kernel, in_specs=[anywhere] * 2, out_specs=pl.B...  5.15 us
    all_gather x1, blocking collectives, body(): everyone = lax.all_gather(row, 'c', axis=0)  3.56 us
    pallas_call x1, Pallas kernels, products(): pl.pallas_call(products_kernel, in_specs=[pl.BlockSpec(memory_space=pltpu...  1.22 us

profile of v8, /device:TPU:1, one launch (start us, length us, event | category | flops | bytes accessed | tf_op | source)
XLA Modules:
  0.0 57.5 jit_solution(12787001382848163775)
XLA Ops:
  0.0 5.2 %channelize.1 = bf16[4,8,5,4,128]{4,3,2,1,0:T(4,128)(2,1)S(1)} custom-call(bf16[128,16384]{1,0:T(8,128)(2,1)} %bitcast.2, f32[56,4096]{1,0:T(8,128)} %constant.2.clone.table_hbm), custom_call_target="tpu_custom_call" | custom-call | tf_op jit(solution)/shard_map/channelize/pallas_call | solution.py:148
  5.2 9.7 %all_to_all.15.recv_ref = bf16[4,8,5,4,128]{4,3,2,1,0:T(4,128)(2,1)S(1)} all-to-all(bf16[4,8,5,4,128]{4,3,2,1,0:T(4,128)(2,1)S(1)} %channelize.1), channel_id=1, replica_groups={{0,32,16,48},{1,33,17,49},{2,34,18,50},{3,35,19,51},{4,36,20,52},{5,37,..., dimensions={0} | all-to-all | bytes 327680 | tf_op jit(solution)/shard_map/all_to_all | solution.py:269
  14.9 0.1 add_row.1
  14.9 29.2 %all_to_all.16.recv_ref = bf16[16,32,128]{2,1,0:T(8,128)(2,1)S(1)} all-to-all(bf16[16,32,128]{2,1,0:T(8,128)(2,1)S(1)} %add_row.1), channel_id=1, replica_groups={{0,192,384,67,259,451,128,320,3,195,387,64,256,448,131,323},{1,193,385,..., dimensions={0} | all-to-all | bytes 262144 | tf_op jit(solution)/shard_map/all_to_all | solution.py:274
  44.2 8.5 %all_to_all.17 = bf16[4,2,128,128]{3,2,1,0:T(8,128)(2,1)S(1)} all-to-all(bf16[4,2,128,128]{3,2,1,0:T(8,128)(2,1)S(1)} %add_line.1), channel_id=1, replica_groups={{0,9,4,13},{1,8,5,12},{2,11,6,15},{3,10,7,14},{16,25,20,29},{17,24,21,2..., dimensions={0} | all-to-all | bytes 524288 | tf_op jit(solution)/shard_map/all_to_all | solution.py:279
  52.7 3.6 %all_gather.3.all_ref = bf16[2,8,128,128]{3,2,1,0:T(8,128)(2,1)S(1)} all-gather(bf16[1,8,128,128]{3,2,1,0:T(8,128)(2,1)S(1)} %bitcast.3), channel_id=1, replica_groups=mesh['zl'=8,'y'=4,'x'=4,'zh'=2,'c'=2] {'c'}, dimensions={0}, use_global_device_ids=true | all-gather | bytes 786432 | tf_op jit(solution)/shard_map/all_gather | solution.py:283
  56.3 1.2 %products.1 = f32[1,2,64,1024]{3,2,1,0:T(8,128)} custom-call(bf16[2,8,128,128]{3,2,1,0:T(8,128)(2,1)S(1)} %all_gather.3.all_ref), custom_call_target="tpu_custom_call" | custom-call | tf_op jit(solution)/shard_map/products/pallas_call | solution.py:253
  (1 shorter events, 0.0 us)
